TPU v7x, 256 devices: a whole 4x4x8 slice. The times are simulated.
256 devices in a mesh: seq: 32 (over z, y), batch: 8 (over x, core).
Axes of the slice: x: 4, y: 4, z: 8, core: 2. Of those that a mesh axis runs over, the one named last changes fastest.
Arguments:
- coarse: bfloat16 [8, 2048, 768], P('batch', 'seq'), may hold values from -6 to 6
- skip: bfloat16 [8, 4096, 768], P('batch', 'seq'), may hold values from -6 to 6
- donor: int32 [8, 4096], P('batch', 'seq'), may hold values from 0 to 4095, as said below
- acceptor: int32 [8, 4096], P('batch', 'seq'), may hold values from 0 to 4095, as said below
- conv_weight: bfloat16 [768, 4, 768], P('seq'), may hold values from -0.15625 to 0.15625
- donor_weight: bfloat16 [768, 768], P('seq'), may hold values from -0.21875 to 0.21875
- acceptor_weight: bfloat16 [768, 768], P('seq'), may hold values from -0.21875 to 0.21875
- track_weight: bfloat16 [768, 367], P('seq'), may hold values from -0.21875 to 0.21875
- gain: bfloat16 [768], P('seq'), may hold values from 0.5 to 1.5
- fine_grad: bfloat16 [8, 4096, 768], P('batch', 'seq'), may hold values from -6 to 6
- score_grad: bfloat16 [8, 4096, 367], P('batch', 'seq'), may hold values from -6 to 6
Outputs:
- scores: bfloat16 [8, 4096, 367], P('batch', 'seq')
- coarse_grad: bfloat16 [8, 2048, 768], P('batch', 'seq')
- skip_grad: bfloat16 [8, 4096, 768], P('batch', 'seq')
- conv_grad: float32 [768, 4, 768], P('seq')
- donor_grad: float32 [768, 768], P('seq')
- acceptor_grad: float32 [768, 768], P('seq')
- track_grad: float32 [768, 367], P('seq')
- gain_grad: float32 [768], P('seq')
Inputs may be any that keep to these rules, and one draw needn't show every extreme that they name: `donor`: the donors of pairs k * 128 to (k + 1) * 128 - 1 of a sequence lie in positions k * 128 to (k + 1) * 128 - 1. A pair's acceptor lies in the block of 128 positions of its donor or in one of the two blocks beside it. Of the 128 pairs of one block, at most 64 have their acceptors in any one block, and for every block of pairs some block receives exactly 64.
All inputs are finite; a program needn't handle non-finite values.
Results may differ from a plain program's by a relative error of at most 0.029.
Values may be sent and summed in bfloat16 or wider, within the bound.
No kernel may reach another device: no remote copies, remote signals or barrier semaphores. Data moves between devices by JAX's collectives and lax.ppermute only.
A program may use at most 128 MiB of HBM per device.

v0:
```python
import jax
import jax.numpy as jnp
from jax import lax
from jax.sharding import PartitionSpec as P


def padded_2(block, sides, width):
    for axis, dim in sides:
        count = lax.axis_size(axis)
        forward = [(i, i + 1) for i in range(count - 1)]
        backward = [(target, source) for source, target in forward]
        low = lax.ppermute(
            lax.slice_in_dim(block, block.shape[dim] - width, None, axis=dim), axis, forward
        )
        high = lax.ppermute(lax.slice_in_dim(block, 0, width, axis=dim), axis, backward)
        block = jnp.concatenate([low, block, high], axis=dim)
    return block


def shifted(block, axis, distance):
    devices = range(lax.axis_size(axis))
    route = [(i - distance, i) for i in devices if i - distance in devices]
    return lax.ppermute(block, axis, route)


def matmul(left_rows, right_rows):
    return jnp.dot(left_rows, right_rows, preferred_element_type=jnp.float32)


def matmul_transposed(left_rows, right_rows):
    return lax.dot_general(
        left_rows, right_rows, (((1,), (1,)), ((), ())), preferred_element_type=jnp.float32
    )


def outer_sum(left_rows, right_rows):
    return lax.dot_general(
        left_rows, right_rows, (((0,), (0,)), ((), ())), preferred_element_type=jnp.float32
    )


def local(
    coarse,
    skip,
    donor,
    acceptor,
    conv_weight,
    donor_weight,
    acceptor_weight,
    track_weight,
    gain,
    fine_grad,
    score_grad,
):
    conv_full, donor_full, acceptor_full, track_full, gain_full = (
        lax.all_gather(conv_weight, "seq", axis=0, tiled=True),
        lax.all_gather(donor_weight, "seq", axis=0, tiled=True),
        lax.all_gather(acceptor_weight, "seq", axis=0, tiled=True),
        lax.all_gather(track_weight, "seq", axis=0, tiled=True),
        lax.all_gather(gain, "seq", axis=0, tiled=True),
    )
    channels = gain_full.shape[0]
    half_rows = coarse.shape[1]
    fine_rows = 2 * half_rows
    conv_flat = conv_full.reshape(channels, 4 * channels)
    gain_f32 = gain_full.astype(jnp.float32)
    padded = padded_2(coarse[0], (("seq", 0),), 1)
    tap_out = matmul(padded, conv_flat)

    def tap_block(tap_index, first_row):
        return tap_out[
            first_row : first_row + half_rows, tap_index * channels : (tap_index + 1) * channels
        ]

    even_rows = tap_block(1, 1) + tap_block(3, 0)
    odd_rows = tap_block(2, 1) + tap_block(0, 2)
    conv_out = jnp.stack([even_rows, odd_rows], 1).reshape(fine_rows, channels)
    pre_norm = conv_out + skip[0].astype(jnp.float32)
    inv_rms = lax.rsqrt(jnp.mean(pre_norm * pre_norm, -1, keepdims=True) + 1e-06)
    hidden = (pre_norm * inv_rms * gain_f32).astype(jnp.bfloat16)
    my_block = lax.axis_index("seq")
    donor_local = donor[0] - my_block * fine_rows
    donor_rows = hidden[donor_local]
    proj_donor = matmul(donor_rows, donor_full).astype(jnp.bfloat16)
    acceptor_pos = acceptor[0]
    pairs_here = acceptor_pos.shape[0]
    slots_per = pairs_here // 2
    owner_block = acceptor_pos // fine_rows
    group_of = owner_block - my_block + 1
    acceptor_local = acceptor_pos - owner_block * fine_rows
    onehot_group = (group_of[:, None] == jnp.arange(3, dtype=jnp.int32)[None, :]).astype(jnp.int32)
    slot_of = jnp.sum((jnp.cumsum(onehot_group, 0) - 1) * onehot_group, 1)
    requests = jnp.zeros((3, slots_per), jnp.int32).at[group_of, slot_of].set(acceptor_local)
    owner_index = [None, requests[1], None]
    rows_back = [None, matmul(hidden[requests[1]], acceptor_full).astype(jnp.bfloat16), None]
    for offset in (-1, 1):
        incoming = shifted(requests[offset + 1], "seq", offset)
        owner_index[offset + 1] = incoming
        answer = matmul(hidden[incoming], acceptor_full).astype(jnp.bfloat16)
        rows_back[offset + 1] = shifted(answer, "seq", -offset)
    proj_acceptor = jnp.stack(rows_back)[group_of, slot_of]
    product = (proj_donor.astype(jnp.float32) * proj_acceptor.astype(jnp.float32)).astype(
        jnp.bfloat16
    )
    scores = matmul(product, track_full).astype(jnp.bfloat16)
    score_rows = score_grad[0]
    grad_product = matmul_transposed(score_rows, track_full)
    grad_donor = (grad_product * proj_acceptor.astype(jnp.float32)).astype(jnp.bfloat16)
    grad_acceptor = (grad_product * proj_donor.astype(jnp.float32)).astype(jnp.bfloat16)
    back_donor = matmul_transposed(grad_donor, donor_full)
    grad_slots = (
        jnp.zeros((3, slots_per, channels), jnp.bfloat16).at[group_of, slot_of].set(grad_acceptor)
    )
    owner_grads = [None, grad_slots[1], None]
    for offset in (-1, 1):
        owner_grads[offset + 1] = shifted(grad_slots[offset + 1], "seq", offset)
    index_all = jnp.concatenate(owner_index, 0)
    grads_all = jnp.concatenate(owner_grads, 0)
    rows_all = hidden[index_all]
    back_acceptor = matmul_transposed(grads_all, acceptor_full)
    grad_hidden = fine_grad[0].astype(jnp.float32).at[donor_local].add(back_donor)
    grad_hidden = grad_hidden.at[index_all].add(back_acceptor)
    scaled = grad_hidden * gain_f32
    cubed = inv_rms * inv_rms * inv_rms
    skip_rows = (
        inv_rms * scaled - pre_norm * cubed * jnp.mean(scaled * pre_norm, -1, keepdims=True)
    ).astype(jnp.bfloat16)
    gain_term = jnp.sum(grad_hidden * pre_norm * inv_rms, 0)
    grad_padded = padded_2(skip_rows, (("seq", 0),), 1)
    core_rows = grad_padded[1:-1].reshape(half_rows, 2, channels)
    even_grad = core_rows[:, 0]
    odd_grad = core_rows[:, 1]
    prev_odd = jnp.concatenate([grad_padded[0:1], odd_grad[:-1]], 0)
    next_even = jnp.concatenate([even_grad[1:], grad_padded[-1:]], 0)
    grad_taps = jnp.concatenate([prev_odd, even_grad, odd_grad, next_even], 1)
    coarse_back = matmul_transposed(grad_taps, conv_flat).astype(jnp.bfloat16)
    centre_cols = padded[1:-1]
    conv_part = jnp.concatenate(
        [
            outer_sum(padded[2:], odd_grad),
            outer_sum(centre_cols, even_grad),
            outer_sum(centre_cols, odd_grad),
            outer_sum(padded[:-2], even_grad),
        ],
        1,
    )
    donor_part = outer_sum(donor_rows, grad_donor)
    acceptor_part = outer_sum(rows_all, grads_all)
    track_part = outer_sum(product, score_rows)
    gain_part = gain_term[:, None]
    joined = jnp.concatenate([conv_part, donor_part, acceptor_part, track_part, gain_part], 1)
    grad_share = lax.psum_scatter(
        lax.optimization_barrier(joined.astype(jnp.bfloat16))
        .astype(jnp.float32)
        .astype(jnp.bfloat16),
        "seq",
        scatter_dimension=0,
        tiled=True,
    )
    grad_total = lax.psum(grad_share, "batch").astype(jnp.float32)
    rescale = float(lax.axis_size("batch") * lax.axis_size("seq") * fine_rows) ** (-0.5)
    grad_total = grad_total * rescale
    tracks_count = track_full.shape[1]
    conv_grad = grad_total[:, : 4 * channels].reshape(-1, 4, channels)
    donor_grad = grad_total[:, 4 * channels : 5 * channels]
    acceptor_grad = grad_total[:, 5 * channels : 6 * channels]
    track_grad = grad_total[:, 6 * channels : 6 * channels + tracks_count]
    gain_grad = grad_total[:, 6 * channels + tracks_count]
    return (
        scores[None],
        coarse_back[None],
        skip_rows[None],
        conv_grad,
        donor_grad,
        acceptor_grad,
        track_grad,
        gain_grad,
    )


def solution(mesh):
    return jax.shard_map(
        local,
        mesh=mesh,
        in_specs=(
            P("batch", "seq", None),
            P("batch", "seq", None),
            P("batch", "seq"),
            P("batch", "seq"),
            P("seq", None, None),
            P("seq", None),
            P("seq", None),
            P("seq", None),
            P("seq"),
            P("batch", "seq", None),
            P("batch", "seq", None),
        ),
        out_specs=(
            P("batch", "seq", None),
            P("batch", "seq", None),
            P("batch", "seq", None),
            P("seq", None, None),
            P("seq", None),
            P("seq", None),
            P("seq", None),
            P("seq"),
        ),
        check_vma=False,
    )
```

profile of v0, /device:TPU:1, one launch (start us, length us, event | category | flops | bytes accessed | tf_op | source)
XLA Modules:
  0.0 615.6 jit_solution(13591040123788144414)
XLA Ops:
  9.5 4.0 collective-permute-start
  16.7 6.4 %scatter_fusion = s32[3,64]{1,0:T(4,128)S(1)} fusion(s32[3,64]{1,0:T(4,128)S(1)} %broadcast_in_dim.17, s32[128]{0:T(128)S(1)} %fusion.40, s32[128]{0:T(128)S(1)} %get-tuple-element.36), kind=kCustom, calls=%fused_computation.6 | custom fusion | bytes 2560 | tf_op jit(solution)/shard_map/scatter | solution.py:93
  23.1 4.0 collective-permute-start.4
  28.6 47.6 %all_gather.19 = bf16[768,367]{1,0:T(8,128)(2,1)S(1)} all-gather(bf16[24,367]{1,0:T(8,128)(2,1)S(1)} %copy-done.14), channel_id=1, replica_groups=mesh['seq'=32,'batch'=8] {'seq'}, dimensions={0}, use_global_device_ids=true | all-gather | bytes 581328 | tf_op jit(solution)/shard_map/all_gather | solution.py:59
  77.7 58.8 %all-reduce = bf16[768]{0:T(1024)(128)(2,1)S(1)} all-reduce(bf16[768]{0:T(1024)(128)(2,1)S(1)} %dynamic-update-slice), channel_id=1, replica_groups=mesh['seq'=32,'batch'=8] {'seq'}, use_global_device_ids=true, to_apply=%add | all-reduce | flops 768 | bytes 3072
  136.7 3.4 copy.52
  144.7 1.4 gather_fusion.2
  146.8 24.5 %all-gather.8.cloned.1.call-done = bf16[768,768]{1,0:T(8,128)(2,1)} async-done(((bf16[24,768]{1,0:T(8,128)(2,1)}), bf16[768,768]{1,0:T(8,128)(2,1)}) %all-gather.8.cloned.1.call-update) | async-done | bytes 1179664 | tf_op jit(solution)/shard_map/all_gather | solution.py:58
  171.3 2.3 convolution_convert_fusion.10
  173.6 2.7 collective-permute-start.3
  179.5 1.7 gather_fusion.5
  181.2 66.9 %all-gather.6.cloned.1.call-done = bf16[768,768]{1,0:T(8,128)(2,1)} async-done(((bf16[24,768]{1,0:T(8,128)(2,1)}), bf16[768,768]{1,0:T(8,128)(2,1)}) %all-gather.6.cloned.1.call-update) | async-done | bytes 1179664 | tf_op jit(solution)/shard_map/all_gather | solution.py:57
  248.1 1.6 fusion.2
  250.8 8.4 %scatter_fusion.2 = bf16[3,64,768]{2,1,0:T(8,128)(2,1)S(1)} fusion(bf16[3,64,768]{2,1,0:T(8,128)(2,1)S(1)} %broadcast_in_dim.21, s32[128]{0:T(128)S(1)} %fusion.40, bf16[128,768]{1,0:T(8,128)(2,1)S(1)} %get-tuple-element.60), kind=kCustom, calls=%fused_computation.8 | custom fusion | bytes 590848 | tf_op jit(solution)/shard_map/scatter | solution.py:112
  261.3 4.6 collective-permute-start.7
  268.1 1.5 gather_fusion.4
  269.7 2.8 convolution_convert_fusion.1
  272.5 1.3 fusion.51
  274.9 2.2 scatter_fusion.1
  277.2 2.3 fusion.24
  279.5 2.6 scatter_fusion.3
  283.9 1.5 fusion
  285.4 1.5 convolution_convert_fusion.5
  287.0 1.6 convolution_convert_fusion.2
  288.5 2.6 convolution_convert_fusion
  291.1 37.3 %concatenate.67 = bf16[768,4976]{0,1:T(8,128)(2,1)} concatenate(bf16[768,768]{0,1:T(8,128)(2,1)} %convolution_convert_fusion.5, bf16[768,768]{0,1:T(8,128)(2,1)} %fusion, bf16[768,768]{0,1:T(8,128)(2,1)S(1)} %fusion.1, bf16[768,768]{0,1:T(8,128)(2,1)} %convolution_convert_fusion.2, bf16[768,768]{0,1:T(8,128)(2,1)} %convolution_convert_fusion.1, ...), dimensions={1} | concatenate | bytes 15286272 | tf_op jit(solution)/shard_map/concatenate | solution.py:151
  329.2 1.4 collective-permute-start.8
  333.2 202.0 %all-reduce.7.cloned.1.call-done = bf16[768,4976]{0,1:T(8,128)(2,1)} async-done(((bf16[768,4976]{0,1:T(8,128)(2,1)}), bf16[768,4976]{0,1:T(8,128)(2,1)}) %all-reduce.7.cloned.1.call-update) | async-done | bytes 7643152
  535.2 3.3 constant_dynamic-slice_fusion
  538.5 4.5 fusion.3
  543.0 60.4 %all-reduce.5.cloned.1.call-done = bf16[24,4976]{0,1:T(8,128)(2,1)} async-done(((bf16[24,4976]{0,1:T(8,128)(2,1)}), bf16[24,4976]{0,1:T(8,128)(2,1)}) %all-reduce.5.cloned.1.call-update) | async-done | bytes 238864 | tf_op jit(solution)/shard_map/psum | solution.py:160
  603.4 1.5 convert_multiply_fusion
  (140 shorter events, 31.2 us)
Async XLA Ops:
  7.2 242.5 %copy-start = (bf16[1,128,367]{1,2,0:T(8,128)(2,1)S(1)}, bf16[1,128,367]{1,2,0:T(8,128)(2,1)}, u32[]{:S(2)}) copy-start(bf16[1,128,367]{1,2,0:T(8,128)(2,1)} %param.21) | copy-start | bytes 281860
  7.2 21.3 %copy-start.23 = (s32[1,128]{1,0:T(1,128)S(1)}, s32[1,128]{1,0:T(1,128)}, u32[]{:S(2)}) copy-start(s32[1,128]{1,0:T(1,128)} %param.13) | copy-start | bytes 1540
  7.2 21.4 %copy-start.13 = (bf16[1,128,768]{2,1,0:T(8,128)(2,1)S(1)}, bf16[1,128,768]{2,1,0:T(8,128)(2,1)}, u32[]{:S(2)}) copy-start(bf16[1,128,768]{2,1,0:T(8,128)(2,1)} %param.20) | copy-start | bytes 589828
  7.2 21.4 %copy-start.14 = (bf16[24,367]{1,0:T(8,128)(2,1)S(1)}, bf16[24,367]{1,0:T(8,128)(2,1)}, u32[]{:S(2)}) copy-start(bf16[24,367]{1,0:T(8,128)(2,1)} %param.18) | copy-start | bytes 52852
  7.2 129.5 %all-gather.4.cloned.1.call-start = ((), (), s32[]{:S(2)}) async-start(), calls=%async_computation | async-start | bytes 4866048 | tf_op jit(solution)/shard_map/all_gather | solution.py:56
  7.9 163.4 %all-gather.8.cloned.1.call-start = ((), (), s32[]{:S(2)}) async-start(), calls=%async_computation.2 | async-start | bytes 1216512 | tf_op jit(solution)/shard_map/all_gather | solution.py:58
  8.7 239.4 %all-gather.6.cloned.1.call-start = ((), (), s32[]{:S(2)}) async-start(), calls=%async_computation.1 | async-start | bytes 1216512 | tf_op jit(solution)/shard_map/all_gather | solution.py:57
  9.5 130.7 %collective-permute-start = (bf16[1,768]{1,0:T(2,128)(2,1)S(1)}, bf16[1,768]{1,0:T(2,128)(2,1)S(1)}, u32[]{:S(2)}, u32[]{:S(2)}) collective-permute-start(bf16[1,768]{1,0:T(2,128)(2,1)S(1)} %get-tuple-element.51), channel_id=1, source_target_pairs={{0,8},{8,16},{16,24},{24,32},{32,40},{40,48},{48,56},{56,64},{64,7... | collective-permute-start | bytes 4616 | tf_op jit(solution)/shard_map/ppermute | solution.py:12
  13.5 126.6 %collective-permute-start.1 = (bf16[1,768]{1,0:T(2,128)(2,1)S(1)}, bf16[1,768]{1,0:T(2,128)(2,1)S(1)}, u32[]{:S(2)}, u32[]{:S(2)}) collective-permute-start(bf16[1,768]{1,0:T(2,128)(2,1)S(1)} %get-tuple-element.52), channel_id=1, source_target_pairs={{8,0},{16,8},{24,16},{32,24},{40,32},{48,40},{56,48},{64,56},{72,6... | collective-permute-start | bytes 4616 | tf_op jit(solution)/shard_map/ppermute | solution.py:15
  16.6 59.5 %copy-start.21 = (u32[256]{0:T(256)S(1)}, u32[256]{0:T(256)}, u32[]{:S(2)}) copy-start(u32[256]{0:T(256)} %constant.113) | copy-start | bytes 3076
  16.6 60.8 %copy-start.24 = (bf16[24]{0:T(256)(128)(2,1)S(1)}, bf16[24]{0:T(256)(128)(2,1)}, u32[]{:S(2)}) copy-start(bf16[24]{0:T(256)(128)(2,1)} %param.19) | copy-start | bytes 148
  23.1 113.4 %collective-permute-start.4 = (s32[64]{0:T(128)S(1)}, s32[64]{0:T(128)S(1)}, u32[]{:S(2)}, u32[]{:S(2)}) collective-permute-start(s32[64]{0:T(128)S(1)} %get-tuple-element.54), channel_id=1, source_target_pairs={{0,8},{8,16},{16,24},{24,32},{32,40},{40,48},{48,56},{56,64},{64,7... | collective-permute-start | bytes 776 | tf_op jit(solution)/shard_map/ppermute | solution.py:23
  27.1 109.5 %collective-permute-start.2 = (s32[64]{0:T(128)S(1)}, s32[64]{0:T(128)S(1)}, u32[]{:S(2)}, u32[]{:S(2)}) collective-permute-start(s32[64]{0:T(128)S(1)} %get-tuple-element.55), channel_id=1, source_target_pairs={{8,0},{16,8},{24,16},{32,24},{40,32},{48,40},{56,48},{64,56},{72,6... | collective-permute-start | bytes 776 | tf_op jit(solution)/shard_map/ppermute | solution.py:23
  28.4 506.8 %all-reduce.7.cloned.1.call-start = ((), (), s32[]{:S(2)}) async-start(), calls=%async_computation.4 | async-start | bytes 15286272
  28.5 111.6 %copy-start.19 = (s32[128]{0:T(128)}, s32[128]{0:T(128)S(1)}, u32[]{:S(2)}) copy-start(s32[128]{0:T(128)S(1)} %fusion.38) | copy-start | bytes 1540
  136.6 3.5 copy-start.15
  136.7 3.5 copy-start.7
  171.3 5.0 copy-start.2
  173.6 93.5 %collective-permute-start.3 = (bf16[64,768]{1,0:T(8,128)(2,1)}, bf16[64,768]{1,0:T(8,128)(2,1)}, u32[]{:S(2)}, u32[]{:S(2)}) collective-permute-start(bf16[64,768]{1,0:T(8,128)(2,1)} %convolution_convert_fusion.10), channel_id=1, source_target_pairs={{0,8},{8,16},{16,24},{24,32},{32,40},{40,48},{48,56},{56,64},{64,7... | collective-permute-start | bytes 294920 | tf_op jit(solution)/shard_map/ppermute | solution.py:23
  177.3 89.9 %collective-permute-start.5 = (bf16[64,768]{1,0:T(8,128)(2,1)}, bf16[64,768]{1,0:T(8,128)(2,1)}, u32[]{:S(2)}, u32[]{:S(2)}) collective-permute-start(bf16[64,768]{1,0:T(8,128)(2,1)} %convolution_convert_fusion.8), channel_id=1, source_target_pairs={{8,0},{16,8},{24,16},{32,24},{40,32},{48,40},{56,48},{64,56},{72,6... | collective-permute-start | bytes 294920 | tf_op jit(solution)/shard_map/ppermute | solution.py:23
  179.5 68.6 %copy-start.9 = (bf16[128,768]{1,0:T(8,128)(2,1)}, bf16[128,768]{1,0:T(8,128)(2,1)S(1)}, u32[]{:S(2)}) copy-start(bf16[128,768]{1,0:T(8,128)(2,1)S(1)} %gather_fusion) | copy-start | bytes 589828
  260.0 17.2 %collective-permute-start.6 = (bf16[64,768]{1,0:T(8,128)(2,1)}, bf16[64,768]{1,0:T(8,128)(2,1)}, u32[]{:S(2)}, u32[]{:S(2)}) collective-permute-start(bf16[64,768]{1,0:T(8,128)(2,1)} %get-tuple-element.42), channel_id=1, source_target_pairs={{8,0},{16,8},{24,16},{32,24},{40,32},{48,40},{56,48},{64,56},{72,6... | collective-permute-start | bytes 294920 | tf_op jit(solution)/shard_map/ppermute | solution.py:23
  261.3 15.9 %collective-permute-start.7 = (bf16[64,768]{1,0:T(8,128)(2,1)}, bf16[64,768]{1,0:T(8,128)(2,1)}, u32[]{:S(2)}, u32[]{:S(2)}) collective-permute-start(bf16[64,768]{1,0:T(8,128)(2,1)} %get-tuple-element.43), channel_id=1, source_target_pairs={{0,8},{8,16},{16,24},{24,32},{32,40},{40,48},{48,56},{56,64},{64,7... | collective-permute-start | bytes 294920 | tf_op jit(solution)/shard_map/ppermute | solution.py:23
  269.6 2.8 copy-start.3
  269.6 2.8 copy-start.4
  279.5 2.6 copy-start.18
  279.5 2.8 copy-start.22
  282.5 46.7 %copy-start.12 = (bf16[128,768]{1,0:T(8,128)(2,1)}, bf16[128,768]{1,0:T(8,128)(2,1)S(1)}, u32[]{:S(2)}) copy-start(bf16[128,768]{1,0:T(8,128)(2,1)S(1)} %subtract_convert_fusion) | copy-start | bytes 589828
  285.4 3.1 copy-start.10
  328.5 275.0 %all-reduce.5.cloned.1.call-start = ((), (), s32[]{:S(2)}) async-start(), calls=%async_computation.3 | async-start | bytes 2547712 | tf_op jit(solution)/shard_map/psum | solution.py:160
  329.2 209.3 %collective-permute-start.8 = (bf16[1,768]{1,0:T(2,128)(2,1)S(1)}, bf16[1,768]{1,0:T(2,128)(2,1)S(1)}, u32[]{:S(2)}, u32[]{:S(2)}) collective-permute-start(bf16[1,768]{1,0:T(2,128)(2,1)S(1)} %get-tuple-element.45), channel_id=1, source_target_pairs={{0,8},{8,16},{16,24},{24,32},{32,40},{40,48},{48,56},{56,64},{64,7... | collective-permute-start | bytes 4616 | tf_op jit(solution)/shard_map/ppermute | solution.py:12
  330.5 207.9 %collective-permute-start.9 = (bf16[1,768]{1,0:T(2,128)(2,1)S(1)}, bf16[1,768]{1,0:T(2,128)(2,1)S(1)}, u32[]{:S(2)}, u32[]{:S(2)}) collective-permute-start(bf16[1,768]{1,0:T(2,128)(2,1)S(1)} %get-tuple-element.46), channel_id=1, source_target_pairs={{8,0},{16,8},{24,16},{32,24},{40,32},{48,40},{56,48},{64,56},{72,6... | collective-permute-start | bytes 4616 | tf_op jit(solution)/shard_map/ppermute | solution.py:15
  (8 other events, 15.8 us)
Sparse Core Ops, SparseCore 0:
  10.6 85.8 all-gather.3
  99.1 72.1 all-gather.7
  173.9 74.1 all-gather.5
  328.6 206.5 all-reduce.6
  538.6 64.8 all-reduce.4
where the time goes:
time: 619 us; the launch traced here: 616 us
  waiting for transfers between devices  355 us (57%)
  blocking collectives  106 us (17%)
  local copies, waits for them, and re-layouts  75.5 us (12%)
  matrix products  28.9 us (5%)
  starting transfers between devices  23.3 us (4%)
  between operations  15.8 us (3%)
  other arithmetic  10.4 us (2%)
    unnamed x6, waiting for transfers between devices  203 us
    all_gather x1, waiting for transfers between devices, local(): lax.all_gather(donor_weight, 'seq', axis=0, tiled=True)  66.9 us
    psum x1, waiting for transfers between devices, local(): grad_total = lax.psum(grad_share, 'batch').astype(jnp.float32)  60.4 us
    unnamed x1, blocking collectives  58.8 us
    all_gather x1, blocking collectives, local(): lax.all_gather(track_weight, 'seq', axis=0, tiled=True)  47.6 us
    concatenate x1, local copies, waits for them, and re-layouts, local(): jnp.concatenate([conv_part, donor_part, acceptor_part, track_part, gain_p...  37.3 us
    all_gather x1, waiting for transfers between devices, local(): lax.all_gather(acceptor_weight, 'seq', axis=0, tiled=True)  24.5 us
    ppermute x6, starting transfers between devices, shifted(): return lax.ppermute(block, axis, route)  15.1 us
  transfers between devices with their start and end apart: 15, of which 4 were waited for; matrix products, arithmetic and copies ran while one was open for 9% of the time, Pallas kernels for 0%

commit v1 on v0

v1 whole, which is shorter than its diff:
```python
import functools

import jax
import jax.numpy as jnp
from jax import lax
from jax.experimental import pallas as pl
from jax.experimental.pallas import tpu as pltpu
from jax.sharding import Mesh
from jax.sharding import PartitionSpec as P

AXES = ("z", "y", "x", "c")
SEQ = ("z", "y")
GROUP = ("x", "c")
BF = jnp.bfloat16
F32 = jnp.float32
CHUNK = 256


def send_seq(block, step):
    count = lax.axis_size(SEQ)
    pairs = [(i, i + step) for i in range(count) if 0 <= i + step < count]
    return lax.ppermute(block, SEQ, pairs)


def send_edge(block, steps):
    sizes = [lax.axis_size(axis) for axis in AXES]
    seqs, per = sizes[0] * sizes[1], sizes[2] * sizes[3]
    pairs = []
    for source in range(seqs):
        for member in range(per):
            step = steps[member // sizes[3]]
            if step and 0 <= source + step < seqs:
                pairs.append((source * per + member, (source + step) * per + member))
    return lax.ppermute(block, AXES, pairs)


def send_x(block, step):
    count = lax.axis_size("x")
    return lax.ppermute(block, "x", [(i, (i + step) % count) for i in range(count)])


def swap_core(block):
    return lax.ppermute(block, "c", [(0, 1), (1, 0)])


def mm(left, right):
    return lax.dot_general(left, right, (((1,), (0,)), ((), ())), preferred_element_type=F32)


def mm_nt(left, right):
    return lax.dot_general(left, right, (((1,), (1,)), ((), ())), preferred_element_type=F32)


def mm_tn(left, right):
    return lax.dot_general(left, right, (((0,), (0,)), ((), ())), preferred_element_type=F32)


def call(body, shapes, *operands, scratch=(), scalars=0):
    vmem = pl.BlockSpec(memory_space=pltpu.VMEM)
    smem = pl.BlockSpec(memory_space=pltpu.SMEM)
    return pl.pallas_call(
        body,
        out_shape=[jax.ShapeDtypeStruct(shape, kind) for shape, kind in shapes],
        in_specs=[smem] * scalars + [vmem] * (len(operands) - scalars),
        out_specs=[vmem] * len(shapes),
        scratch_shapes=[pltpu.VMEM(shape, kind) for shape, kind in scratch],
        compiler_params=pltpu.CompilerParams(vmem_limit_bytes=16 * 1024 * 1024),
    )(*operands)


def split_hot(rows, transposed):
    row = lax.broadcasted_iota(jnp.int32, (rows, rows), 0)
    column = lax.broadcasted_iota(jnp.int32, (rows, rows), 1)
    if transposed:
        row, column = column, row
    hot = (row % 2) * (rows // 2) + row // 2 == column
    return jnp.where(hot, 1.0, 0.0).astype(BF)


def inverse(pre):
    return lax.rsqrt(jnp.mean(pre * pre, -1, keepdims=True) + 1e-06)


def start_body(
    place_ref, conv_ref, donor_ref, acceptor_ref, track_ref, gain_ref, coarse_ref, out_ref, own_ref
):
    x, c = place_ref[0], place_ref[1]
    half = out_ref.shape[1] - CHUNK
    half_rows = coarse_ref.shape[0]
    own_ref[:half_rows] = coarse_ref[...]
    own_ref[half_rows:] = jnp.zeros_like(own_ref[half_rows:])
    depth = out_ref.shape[0]
    for member in range(8):
        tap, part = member // 2, member % 2

        @pl.when((x == tap) & (c == part))
        def _():
            out_ref[:, :half] = conv_ref[:, tap, part * half : (part + 1) * half]
            if member == 7:
                tracks = track_ref.shape[1]
                pad = jnp.zeros((depth, 2 * CHUNK - tracks - 1), BF)
                out_ref[:, half:] = jnp.concatenate([track_ref[:, CHUNK:], gain_ref[...], pad], 1)
            else:
                source = (donor_ref, acceptor_ref, track_ref)[member // 3]
                first = (member % 3) * CHUNK
                out_ref[:, half:] = source[:, first : first + CHUNK]


def norm_body(taps_ref, skip_ref, pre_ref, unit_ref):
    def tap(index):
        return taps_ref[index].astype(F32)

    half_rows = taps_ref.shape[1]
    half = taps_ref.shape[2]
    skip = mm(split_hot(2 * half_rows, True), skip_ref[...])
    pre_ref[:half_rows, :half] = tap(2) + tap(6) + skip[:half_rows, :half]
    pre_ref[:half_rows, half:] = tap(3) + tap(7) + skip[:half_rows, half:]
    pre_ref[half_rows:, :half] = tap(4) + tap(0) + skip[half_rows:, :half]
    pre_ref[half_rows:, half:] = tap(5) + tap(1) + skip[half_rows:, half:]
    pre = pre_ref[...]
    unit_ref[...] = (pre * inverse(pre)).astype(BF)


def one_hot(mask):
    return jnp.where(mask, 1.0, 0.0).astype(BF)


def pair_body(
    pre_ref, chunks_ref, low_ref, high_ref, donor_ref, place_ref, group_ref, group_row_ref, score_ref,
    hidden_ref, product_ref, to_low_ref, to_high_ref, place_donor_ref, own_ref, gain_ref,
    grad_donor_ref, grad_acceptor_ref,
):
    pre = pre_ref[...]
    rows = pre.shape[0]
    slots = rows // 2
    gains = mm_nt(gain_hot(score_ref.shape[1] - CHUNK), chunks_ref[7])
    gain = gains[:1]
    gain_ref[...] = gains
    hidden = (pre * inverse(pre) * gain).astype(BF)
    hidden_ref[...] = hidden
    near = [(ref[...].astype(F32) * gain).astype(BF) for ref in (low_ref, high_ref)]
    lanes = lax.broadcasted_iota(jnp.int32, (rows, rows), 1)
    group = group_ref[...]
    at_place = place_ref[...] == lanes
    donor_hot = one_hot(donor_ref[...] == lanes)
    own_hot = one_hot(at_place & (group == 0))
    pick = jnp.concatenate(
        [own_hot, one_hot(at_place & (group == -1)), one_hot(at_place & (group == 1))], 1
    )
    donor_rows = mm(donor_hot, hidden).astype(BF)
    acceptor_rows = mm(pick, jnp.concatenate([hidden] + near, 0)).astype(BF)
    score = score_ref[...]
    tracks = score.shape[1]
    for index in range(3):
        cols = slice(index * CHUNK, (index + 1) * CHUNK)
        proj_donor = mm(donor_rows, chunks_ref[index]).astype(BF).astype(F32)
        proj_acceptor = mm(acceptor_rows, chunks_ref[3 + index]).astype(BF).astype(F32)
        grad = mm_nt(score[:, :CHUNK], chunks_ref[6, cols]) + mm_nt(
            score[:, CHUNK:], chunks_ref[7, cols, : tracks - CHUNK]
        )
        product_ref[:, cols] = (proj_donor * proj_acceptor).astype(BF)
        grad_donor_ref[:, cols] = (grad * proj_acceptor).astype(BF)
        grad_acceptor_ref[:, cols] = (grad * proj_donor).astype(BF)
    grad_acceptor = grad_acceptor_ref[...]
    before = lax.broadcasted_iota(jnp.int32, (rows, rows), 0) > lanes
    same = group == group_row_ref[...]
    slot_of = jnp.sum(jnp.where(before & same, 1.0, 0.0), 1, keepdims=True).astype(jnp.int32)
    slot_lanes = lax.broadcasted_iota(jnp.int32, (rows, slots), 1)
    numbers = (place_ref[...] + 1).astype(F32)
    first = lax.broadcasted_iota(jnp.int32, (16, rows), 0) == 0
    for which, ref in ((-1, to_low_ref), (1, to_high_ref)):
        hot = (slot_of == slot_lanes) & (group == which)
        ref[:slots] = mm_tn(one_hot(hot), grad_acceptor).astype(BF)
        index_row = jnp.sum(jnp.where(hot, numbers, 0.0), 0, keepdims=True)
        index_row = jnp.concatenate([index_row, jnp.zeros((1, rows - slots), F32)], 1)
        ref[slots:] = jnp.zeros_like(ref[slots:])
        ref[slots:, :rows] = jnp.where(first, index_row, 0.0).astype(BF)
    place_donor_ref[...] = mm_tn(donor_hot, grad_donor_ref[...]).astype(BF)
    own_ref[...] = mm_tn(own_hot, grad_acceptor)


def gain_hot(column):
    return one_hot(lax.broadcasted_iota(jnp.int32, (16, CHUNK), 1) == column)


def base_body(product_ref, chunks_ref, place_ref, fine_ref, scores_ref, base_ref):
    rows = fine_ref.shape[0]
    product = product_ref[...]
    tracks = scores_ref.shape[1]
    scores_ref[:, :CHUNK] = mm(product, chunks_ref[6]).astype(BF)
    scores_ref[:, CHUNK:] = mm(product, chunks_ref[7])[:, : tracks - CHUNK].astype(BF)
    place = place_ref[...]
    total = mm(split_hot(rows, True), fine_ref[...])
    for index in range(3):
        total = total + mm_nt(place[:, index * CHUNK : (index + 1) * CHUNK], chunks_ref[index])
    base_ref[...] = total


def skip_body(
    base_ref, own_ref, chunks_ref, low_ref, high_ref, pre_ref, gain_ref, place_ref, score_ref,
    skip_ref, out_ref,
):
    rows = pre_ref.shape[0]
    half_rows = rows // 2
    channels = pre_ref.shape[1]
    half = channels // 2
    acceptor = own_ref[...]
    numbers = lax.broadcasted_iota(jnp.int32, (rows, half_rows), 0) + 1
    for ref in (low_ref, high_ref):
        asked = ref[half_rows:, :rows].astype(F32)[:1, :half_rows].astype(jnp.int32)
        acceptor = acceptor + mm(one_hot(numbers == asked), ref[:half_rows])
    acceptor = acceptor.astype(BF)
    grad = base_ref[...]
    for index in range(3):
        grad = grad + mm_nt(
            acceptor[:, index * CHUNK : (index + 1) * CHUNK], chunks_ref[3 + index]
        )
    pre = pre_ref[...]
    inv = inverse(pre)
    scaled = grad * gain_ref[:1]
    mean = jnp.mean(scaled * pre, -1, keepdims=True)
    skip = (inv * scaled - pre * (inv * inv * inv) * mean).astype(BF)
    skip_ref[...] = mm(split_hot(rows, False), skip).astype(BF)
    gains = jnp.sum(grad * pre * inv, 0, keepdims=True)
    row = lax.broadcasted_iota(jnp.int32, (half_rows, 128), 0)
    gain_block = jnp.zeros((half_rows, 128), F32)
    for index in range(channels // 128):
        gain_block = jnp.where(row == index, gains[:, index * 128 : (index + 1) * 128], gain_block)
    for index in range(8):
        start = half_rows if (index // 2) % 2 == 0 else 0
        part = (index % 2) * half
        out_ref[index, :, :half] = skip[start : start + half_rows, part : part + half]
        if index == 7:
            tracks = score_ref.shape[1]
            wide = jnp.zeros((rows, 2 * CHUNK - tracks), BF)
            block = jnp.concatenate([score_ref[:, CHUNK:], wide], 1)
        elif index == 6:
            block = score_ref[:, :CHUNK]
        elif index < 3:
            block = place_ref[:, index * CHUNK : (index + 1) * CHUNK]
        else:
            block = acceptor[:, (index - 3) * CHUNK : (index - 2) * CHUNK]
        out_ref[index, :, half : half + CHUNK] = block[:half_rows]
        out_ref[index, :, half + CHUNK :] = block[half_rows:]
    out_ref[7, :, half + 128 : half + CHUNK] = gain_block.astype(BF)


def partial_body(place_ref, left_ref, near_ref, far_ref, grads_ref, out_ref, rows_ref, right_ref):
    x, c = place_ref[0], place_ref[1]
    members, half_rows, _ = grads_ref.shape
    half = left_ref.shape[1] // 2
    rows = 2 * half_rows
    for member in range(members):
        span = pl.ds(member * rows, rows)
        step = lax.rem(x - member // 2 + 4, 4)

        @pl.when(c == member % 2)
        def _():
            rows_ref[span] = near_ref[step]

        @pl.when(c != member % 2)
        def _():
            rows_ref[span] = far_ref[step]

        right_ref[member * rows : member * rows + half_rows] = grads_ref[member, :, half : half + CHUNK]
        right_ref[member * rows + half_rows : (member + 1) * rows] = grads_ref[member, :, half + CHUNK :]
    taps = grads_ref[:, :, :half].reshape(members * half_rows, half)
    wide_y, wide_z, depth, _ = out_ref.shape

    def store(values, columns):
        for z in range(wide_z):
            for y in range(wide_y):
                row = (z * wide_y + y) * depth
                out_ref[y, z, :, columns] = values[row : row + depth].astype(BF)

    store(mm_tn(left_ref[...], taps), slice(0, half))
    rest = mm_tn(rows_ref[...], right_ref[...])
    total = jnp.sum(grads_ref[:, :16, half + 128 : half + CHUNK].astype(F32), 0)
    row = lax.broadcasted_iota(jnp.int32, (128, 128), 0)
    lane = lax.broadcasted_iota(jnp.int32, (128, 128), 1)
    ones = jnp.ones((128, 128), BF)
    gains = [
        mm(jnp.where(row == lane, total[index : index + 1], 0.0).astype(BF), ones)
        for index in range(2 * half // 128)
    ]
    store(rest[:, :128], slice(half, half + 128))
    gain_last = (x == 3) & (c == 1)
    store(
        jnp.where(gain_last, jnp.concatenate(gains, 0), rest[:, 128:]),
        slice(half + 128, half + CHUNK),
    )


def final_body(rescale, shares_ref, conv_ref, donor_ref, acceptor_ref, track_ref, gain_ref):
    half = conv_ref.shape[2] // 2
    tracks = track_ref.shape[1]
    for member in range(8):
        values = shares_ref[member].astype(F32) * rescale
        tap, part = member // 2, member % 2
        conv_ref[:, tap, part * half : (part + 1) * half] = values[:, :half]
        if member == 7:
            track_ref[:, CHUNK:] = values[:, half : half + tracks - CHUNK]
            gain_ref[...] = values[:, half + CHUNK // 2 : half + CHUNK // 2 + 1]
        else:
            target = (donor_ref, acceptor_ref, track_ref)[member // 3]
            first = (member % 3) * CHUNK
            target[:, first : first + CHUNK] = values[:, half:]


def local(
    coarse,
    skip,
    donor,
    acceptor,
    conv_weight,
    donor_weight,
    acceptor_weight,
    track_weight,
    gain,
    fine_grad,
    score_grad,
):
    rows_in, _, channels = conv_weight.shape
    half_rows = coarse.shape[1]
    fine_rows = 2 * half_rows
    pairs = donor.shape[1]
    slots = pairs // 2
    tracks = track_weight.shape[1]
    half = channels // 2
    nz, ny, nx, nc = (lax.axis_size(axis) for axis in AXES)
    group_size = nx * nc
    seqs = nz * ny
    seq = lax.axis_index(SEQ)
    batch = lax.axis_index(GROUP)
    x, c = lax.axis_index("x"), lax.axis_index("c")

    place = jnp.stack([x, c])
    both, own = call(
        start_body,
        [((rows_in, half + CHUNK), BF), ((half_rows + 32, channels), BF)],
        place, conv_weight, donor_weight, acceptor_weight, track_weight, gain[:, None], coarse[0],
        scalars=1,
    )
    both = jnp.broadcast_to(both[None], (nz, rows_in, half + CHUNK))
    both = lax.all_to_all(both, "z", 0, 0, tiled=True)

    def over_y(block):
        block = jnp.broadcast_to(block[None], (ny,) + block.shape)
        block = lax.all_to_all(block, "y", 0, 0, tiled=True)
        return jnp.swapaxes(block, 0, 1).reshape(channels, block.shape[-1])

    gathered = over_y(both)
    conv_w = gathered[:, :half]
    chunks = lax.all_gather(gathered[:, half:], GROUP, axis=0)

    left_all = lax.all_gather(own, GROUP, axis=0)[:, :half_rows]
    edge = jnp.where(x == 0, left_all[:, 0], left_all[:, half_rows - 1])
    edge = send_edge(edge, (-1, 0, 0, 1))[:, None]
    wide_rows = jnp.concatenate([edge, left_all, edge], 1)
    first_row = jnp.where(x == 0, 2, jnp.where(x == nx - 1, 0, 1))
    left_rows = lax.dynamic_slice_in_dim(wide_rows, first_row, half_rows, 1)
    left_rows = left_rows.reshape(-1, channels)

    tap_out = mm(left_rows, conv_w).astype(BF).reshape(group_size, half_rows, half)
    taps = lax.all_to_all(tap_out, GROUP, 0, 0, tiled=True)

    def split_place(place):
        return (place % 2) * half_rows + place // 2

    donor_place = split_place(donor[0] - seq * fine_rows)[:, None]
    owner = acceptor[0] // fine_rows
    group = owner - seq
    acceptor_place = split_place(acceptor[0] - owner * fine_rows)[:, None]

    fine_shape = (fine_rows, channels)
    sent_shape = (slots + 16, channels)
    pre_norm, unit = call(norm_body, [(fine_shape, F32), (fine_shape, BF)], taps, skip[0])
    near_high = send_seq(unit, -1)
    near_low = send_seq(unit, 1)
    hidden, product, to_low, to_high, place_donor, own_grads, gain_rows = call(
        pair_body,
        [(fine_shape, BF), (fine_shape, BF), (sent_shape, BF), (sent_shape, BF), (fine_shape, BF)]
        + [(fine_shape, F32), ((16, channels), F32)],
        pre_norm, chunks, near_low, near_high, donor_place, acceptor_place, group[:, None], group[None, :],
        score_grad[0],
        scratch=[(fine_shape, BF), (fine_shape, BF)],
    )
    grads_high = send_seq(to_low, -1)
    grads_low = send_seq(to_high, 1)
    is_track = [(x + step) % nx == nx - 1 for step in range(nx)]
    left_near = [jnp.where(last, product, hidden) for last in is_track]
    left_near = jnp.stack(
        left_near[:1] + [send_x(left_near[step], step) for step in range(1, nx)], 0
    )
    scores, base = call(
        base_body, [((pairs, tracks), BF), (fine_shape, F32)], product, chunks, place_donor, fine_grad[0]
    )
    skip_out, outgoing = call(
        skip_body,
        [(fine_shape, BF), ((group_size, half_rows, half + 2 * CHUNK), BF)],
        base, own_grads, chunks, grads_low, grads_high, pre_norm, gain_rows, place_donor, score_grad[0],
    )
    outgoing, left_near = lax.optimization_barrier((outgoing, left_near))
    left_far = swap_core(left_near)
    grads = lax.all_to_all(outgoing, GROUP, 0, 0, tiled=True)
    tap_grads = grads[:, :, :half]
    grad_edge = jnp.where(x == 0, tap_grads[:, half_rows - 1], tap_grads[:, 0])
    grad_edge = send_edge(grad_edge, (1, 0, 0, -1))[:, None]
    (partials,) = call(
        partial_body,
        [((ny, nz, rows_in, half + CHUNK), BF)],
        place, left_rows, left_near, left_far, grads,
        scratch=[((group_size * fine_rows, channels), BF), ((group_size * fine_rows, CHUNK), BF)],
        scalars=1,
    )
    wide_grads = jnp.concatenate([grad_edge, tap_grads, grad_edge], 1)
    first_grad = jnp.where(x == 0, 0, jnp.where(x == nx - 1, 2, 1))
    moved = lax.dynamic_slice_in_dim(wide_grads, first_grad, half_rows, 1).reshape(-1, half)
    back = mm_nt(moved, conv_w).astype(BF).reshape(group_size, half_rows, channels)
    partials, back = lax.optimization_barrier((partials, back))
    coarse_back = lax.psum_scatter(back, GROUP, scatter_dimension=0, tiled=True)
    shares = lax.all_to_all(partials, "y", 0, 0, tiled=True)
    shares = jnp.sum(shares.astype(F32), 0).astype(BF)
    shares = lax.all_to_all(shares, "z", 0, 0, tiled=True)
    shares, coarse_back = lax.optimization_barrier((shares, coarse_back))
    shares = jnp.sum(shares.astype(F32), 0).astype(BF)
    shares = jnp.broadcast_to(shares[None], (group_size,) + shares.shape)
    shares = lax.all_to_all(shares, GROUP, 0, 0, tiled=True)

    rescale = float(group_size * seqs * fine_rows) ** (-0.5)
    conv_grad, donor_grad, acceptor_grad, track_grad, gain_grad = call(
        functools.partial(final_body, rescale),
        [((rows_in, nx, channels), F32), ((rows_in, channels), F32), ((rows_in, channels), F32)]
        + [((rows_in, tracks), F32), ((rows_in, 1), F32)],
        shares,
    )
    gain_grad = gain_grad[:, 0]
    return (
        scores[None],
        coarse_back,
        skip_out[None],
        conv_grad,
        donor_grad,
        acceptor_grad,
        track_grad,
        gain_grad,
    )


def solution(mesh):
    wide = Mesh(mesh.devices.reshape(8, 4, 4, 2), AXES)
    return jax.shard_map(
        local,
        mesh=wide,
        in_specs=(
            P(GROUP, SEQ, None),
            P(GROUP, SEQ, None),
            P(GROUP, SEQ),
            P(GROUP, SEQ),
            P(SEQ, None, None),
            P(SEQ, None),
            P(SEQ, None),
            P(SEQ, None),
            P(SEQ),
            P(GROUP, SEQ, None),
            P(GROUP, SEQ, None),
        ),
        out_specs=(
            P(GROUP, SEQ, None),
            P(GROUP, SEQ, None),
            P(GROUP, SEQ, None),
            P(SEQ, None, None),
            P(SEQ, None),
            P(SEQ, None),
            P(SEQ, None),
            P(SEQ),
        ),
        check_vma=False,
    )
```

time: 619 us -> 197 us (0.32)
  waiting for transfers between devices: 355 us -> 43.6 us
  local copies, waits for them, and re-layouts: 75.5 us -> 13.8 us
  blocking collectives: 106 us -> 68.5 us
  matrix products: 28.9 us -> 2.83 us
  starting transfers between devices: 23.3 us -> 42.3 us
  Pallas kernels: 0 us -> 8.22 us
  other arithmetic: 10.4 us -> 2.32 us
    unnamed x6 -> x3, waiting for transfers between devices: 203 us -> 0.05 us
    all_gather x3 -> x2, waiting for transfers between devices: 91.4 us -> 0.02 us  [the longest x1 0.02 us: local(): left_all = lax.all_gather(own, GROUP, axis=0)[:, :half_rows]]
    all_to_all x0 -> x4, blocking collectives: none -> 68.5 us  [the longest x1 18.8 us: local(): both = lax.all_to_all(both, 'z', 0, 0, tiled=True)]
    psum x1 -> x0, waiting for transfers between devices: 60.4 us -> none  [local(): grad_total = lax.psum(grad_share, 'batch').astype(jnp.float32)]
    unnamed x1 -> x0, blocking collectives: 58.8 us -> none
    all_gather x1 -> x0, blocking collectives: 47.6 us -> none  [local(): lax.all_gather(track_weight, 'seq', axis=0, tiled=True)]
    concatenate x1 -> x0, local copies, waits for them, and re-layouts: 37.3 us -> none  [local(): jnp.concatenate([conv_part, donor_part, acceptor_part, track_part, gain_p...]
    all_to_all x0 -> x3, waiting for transfers between devices: none -> 31.1 us  [the longest x1 13.6 us: local(): grads = lax.all_to_all(outgoing, GROUP, 0, 0, tiled=True)]
  transfers between devices with their start and end apart: 15 -> 16, of which waited for: 4 -> 8; matrix products, arithmetic and copies ran while one was open for 9% -> 3% of each run, Pallas kernels for 0% -> 2%
where the time goes in v1:
time: 197 us; the launch traced here: 196 us
  blocking collectives  68.5 us (35%)
  waiting for transfers between devices  43.6 us (22%)
  starting transfers between devices  42.3 us (21%)
  between operations  14.2 us (7%)
  local copies, waits for them, and re-layouts  13.8 us (7%)
  Pallas kernels  8.22 us (4%)
  matrix products  2.83 us (1%)
  other arithmetic  2.32 us (1%)
    all_to_all x1, blocking collectives, local(): both = lax.all_to_all(both, 'z', 0, 0, tiled=True)  18.8 us
    all_to_all x1, blocking collectives, local(): shares = lax.all_to_all(partials, 'y', 0, 0, tiled=True)  18 us
    all_to_all x1, blocking collectives, local(): shares = lax.all_to_all(shares, 'z', 0, 0, tiled=True)  16.1 us
    all_to_all x1, blocking collectives, over_y(): block = lax.all_to_all(block, 'y', 0, 0, tiled=True)  15.6 us
    all_to_all x1, waiting for transfers between devices, local(): grads = lax.all_to_all(outgoing, GROUP, 0, 0, tiled=True)  13.6 us
    all_to_all x1, waiting for transfers between devices, local(): taps = lax.all_to_all(tap_out, GROUP, 0, 0, tiled=True)  11.9 us
    ppermute x4, waiting for transfers between devices, send_seq(): return lax.ppermute(block, SEQ, pairs)  9.82 us
    ppermute x4, starting transfers between devices, send_seq(): return lax.ppermute(block, SEQ, pairs)  9.08 us
  transfers between devices with their start and end apart: 16, of which 8 were waited for; matrix products, arithmetic and copies ran while one was open for 3% of the time, Pallas kernels for 2%

profile of v1, /device:TPU:1, one launch (start us, length us, event | category | flops | bytes accessed | tf_op | source)
XLA Modules:
  0.0 195.8 jit_solution(1656759786254230855)
XLA Ops:
  8.0 0.9 copy-done.6
  12.1 1.3 shard_map.170
  13.5 18.8 %all_to_all.35 = bf16[8,24,640]{2,1,0:T(8,128)(2,1)S(1)} all-to-all(bf16[8,24,640]{2,1,0:T(8,128)(2,1)S(1)} %broadcast_in_dim.18), channel_id=1, replica_groups=mesh['z'=8,'y'=4,'x'=4,'c'=2] {'z'}, dimensions={0} | all-to-all | bytes 491520 | tf_op jit(solution)/shard_map/all_to_all | solution.py:345
  32.4 15.6 %all_to_all.36 = bf16[4,8,24,640]{3,2,1,0:T(8,128)(2,1)S(1)} all-to-all(bf16[4,8,24,640]{3,2,1,0:T(8,128)(2,1)S(1)} %broadcast_in_dim.19), channel_id=1, replica_groups=mesh['z'=8,'y'=4,'x'=4,'c'=2] {'y'}, dimensions={0} | all-to-all | bytes 1966080 | tf_op jit(solution)/shard_map/all_to_all | solution.py:349
  49.0 1.0 fusion.23
  50.0 1.3 collective-permute-start
  51.3 1.2 slice.38
  52.5 1.9 collective-permute-done
  55.2 1.3 convolution_convert_fusion.1
  56.6 8.2 %all-to-all-start.2 = ((bf16[8,64,384]{2,1,0:T(8,128)(2,1)}), bf16[8,64,384]{2,1,0:T(8,128)(2,1)S(1)}, u32[]{:S(2)}, u32[]{:S(2)}) async-start(bf16[8,64,384]{2,1,0:T(8,128)(2,1)} %bitcast.10), calls=%async_computation.2 | async-start | bytes 786432 | tf_op jit(solution)/shard_map/all_to_all | solution.py:365
  65.4 11.9 %all-to-all-done.2.taps_ref = bf16[8,64,384]{2,1,0:T(8,128)(2,1)S(1)} async-done(((bf16[8,64,384]{2,1,0:T(8,128)(2,1)}), bf16[8,64,384]{2,1,0:T(8,128)(2,1)S(1)}, u32[]{:S(2)}, u32[]{:S(2)}) %all-to-all-start.2) | async-done | bytes 393248 | tf_op jit(solution)/shard_map/all_to_all | solution.py:365
  77.6 2.9 %collective-permute-start.1 = (bf16[128,768]{1,0:T(8,128)(2,1)S(1)}, bf16[128,768]{1,0:T(8,128)(2,1)S(1)}, u32[]{:S(2)}, u32[]{:S(2)}) collective-permute-start(bf16[128,768]{1,0:T(8,128)(2,1)S(1)} %get-tuple-element.37), channel_id=1, source_target_pairs={{0,8},{8,16},{16,24},{24,32},{32,40},{40,48},{48,56},{56,64},{64,7... | collective-permute-start | bytes 589832 | tf_op jit(solution)/shard_map/ppermute | solution.py:22
  80.5 1.3 collective-permute-start.2
  81.8 1.9 collective-permute-done.1.low_ref
  83.8 3.8 %collective-permute-done.2.high_ref = bf16[128,768]{1,0:T(8,128)(2,1)S(1)} collective-permute-done((bf16[128,768]{1,0:T(8,128)(2,1)S(1)}, bf16[128,768]{1,0:T(8,128)(2,1)S(1)}, u32[]{:S(2)}, u32[]{:S(2)}) %collective-permute-start.2) | collective-permute-done | bytes 196640 | tf_op jit(solution)/shard_map/ppermute | solution.py:22
  87.6 1.9 copy-done
  89.5 1.3 shard_map.172
  90.9 1.5 collective-permute-start.7
  93.1 3.6 %collective-permute-start.3 = (bf16[80,768]{1,0:T(8,128)(2,1)S(1)}, bf16[80,768]{1,0:T(8,128)(2,1)S(1)}, u32[]{:S(2)}, u32[]{:S(2)}) collective-permute-start(bf16[80,768]{1,0:T(8,128)(2,1)S(1)} %get-tuple-element.43), channel_id=1, source_target_pairs={{0,8},{8,16},{16,24},{24,32},{32,40},{40,48},{48,56},{56,64},{64,7... | collective-permute-start | bytes 368648 | tf_op jit(solution)/shard_map/ppermute | solution.py:22
  96.7 1.3 collective-permute-start.4
  98.7 4.1 %collective-permute-done.4.high_ref = bf16[80,768]{1,0:T(8,128)(2,1)S(1)} collective-permute-done((bf16[80,768]{1,0:T(8,128)(2,1)S(1)}, bf16[80,768]{1,0:T(8,128)(2,1)S(1)}, u32[]{:S(2)}, u32[]{:S(2)}) %collective-permute-start.4) | collective-permute-done | bytes 122912 | tf_op jit(solution)/shard_map/ppermute | solution.py:22
  102.8 2.0 %shard_map.174 = (bf16[128,768]{1,0:T(8,128)(2,1)}, bf16[8,64,896]{2,1,0:T(8,128)(2,1)}) custom-call(f32[128,768]{1,0:T(8,128)S(1)} %get-tuple-element.41.base_ref, f32[128,768]{1,0:T(8,128)S(1)} %get-tuple-element.42.own_ref, bf16[8,768,256]{2,1,0:T(8,128)(2,1)S(1)} %bitcast.37, bf16[80,768]{1,0:T(8,128)(2,1)S(1)} %collective-permute-done.3.low_ref, ...), custom_call_target="tpu_custom_call" | custom-call | tf_op jit(solution)/shard_map/pallas_call | solution.py:61
  104.9 8.2 %all-to-all-start.3 = ((bf16[8,64,896]{2,1,0:T(8,128)(2,1)}), bf16[8,64,896]{2,1,0:T(8,128)(2,1)S(1)}, u32[]{:S(2)}, u32[]{:S(2)}) async-start(bf16[8,64,896]{2,1,0:T(8,128)(2,1)} %get-tuple-element.49), calls=%async_computation.3 | async-start | bytes 1835008 | tf_op jit(solution)/shard_map/all_to_all | solution.py:405
  113.3 13.6 %all-to-all-done.3.grads_ref = bf16[8,64,896]{2,1,0:T(8,128)(2,1)S(1)} async-done(((bf16[8,64,896]{2,1,0:T(8,128)(2,1)}), bf16[8,64,896]{2,1,0:T(8,128)(2,1)S(1)}, u32[]{:S(2)}, u32[]{:S(2)}) %all-to-all-start.3) | async-done | bytes 917536 | tf_op jit(solution)/shard_map/all_to_all | solution.py:405
  126.9 5.4 %collective-permute-start.9 = (bf16[8,384]{1,0:T(8,128)(2,1)S(1)}, bf16[8,384]{1,0:T(8,128)(2,1)S(1)}, u32[]{:S(2)}, u32[]{:S(2)}) collective-permute-start(bf16[8,384]{1,0:T(8,128)(2,1)S(1)} %bitcast.57), channel_id=1, source_target_pairs={{0,8},{1,9},{8,16},{9,17},{14,6},{15,7},{16,24},{17,25},{22,14},{2... | collective-permute-start | bytes 18440 | tf_op jit(solution)/shard_map/ppermute | solution.py:34
  133.2 1.1 copy-done.3
  134.4 1.8 shard_map.175
  136.6 1.5 convolution_convert_fusion
  138.1 18.0 %all_to_all.37 = bf16[4,8,24,640]{3,2,1,0:T(8,128)(2,1)S(1)} all-to-all(bf16[4,8,24,640]{3,2,1,0:T(8,128)(2,1)S(1)} %shard_map.175), channel_id=1, replica_groups=mesh['z'=8,'y'=4,'x'=4,'c'=2] {'y'}, dimensions={0} | all-to-all | bytes 1966080 | tf_op jit(solution)/shard_map/all_to_all | solution.py:422
  156.2 16.1 %all_to_all.38 = bf16[8,24,640]{2,1,0:T(8,128)(2,1)S(1)} all-to-all(bf16[8,24,640]{2,1,0:T(8,128)(2,1)S(1)} %reduce_sum.24), channel_id=1, replica_groups=mesh['z'=8,'y'=4,'x'=4,'c'=2] {'z'}, dimensions={0} | all-to-all | bytes 491520 | tf_op jit(solution)/shard_map/all_to_all | solution.py:424
  173.8 7.7 %all-to-all-start.6 = ((bf16[8,24,640]{2,1,0:T(8,128)(2,1)}), bf16[8,24,640]{2,1,0:T(8,128)(2,1)S(1)}, u32[]{:S(2)}, u32[]{:S(2)}) async-start(bf16[8,24,640]{2,1,0:T(8,128)(2,1)} %broadcast_in_dim.44), calls=%async_computation.7 | async-start | bytes 491520 | tf_op jit(solution)/shard_map/all_to_all | solution.py:428
  182.2 5.6 %all-to-all-done.6.shares_ref = bf16[8,24,640]{2,1,0:T(8,128)(2,1)S(1)} async-done(((bf16[8,24,640]{2,1,0:T(8,128)(2,1)}), bf16[8,24,640]{2,1,0:T(8,128)(2,1)S(1)}, u32[]{:S(2)}, u32[]{:S(2)}) %all-to-all-start.6) | async-done | bytes 245792 | tf_op jit(solution)/shard_map/all_to_all | solution.py:428
  (81 shorter events, 13.5 us)
Async XLA Ops:
  7.2 41.8 %all-gather.5.cloned.1.call-start = ((), (), s32[]{:S(2)}) async-start(), calls=%async_computation.9 | async-start | bytes 1327104 | tf_op jit(solution)/shard_map/all_gather | solution.py:356
  8.0 0.9 copy-start.6
  9.0 0.9 copy-start.9
  9.8 0.8 copy-start.10
  13.4 74.2 %all-gather.7.cloned.1.call-start = ((), (), s32[]{:S(2)}) async-start(), calls=%async_computation.10 | async-start | bytes 3538944 | tf_op jit(solution)/shard_map/all_gather | solution.py:354
  48.1 7.1 %copy-start.13 = (bf16[4,8,24,640]{3,2,0,1:T(8,128)(2,1)}, bf16[4,8,24,640]{3,2,0,1:T(8,128)(2,1)S(1)}, u32[]{:S(2)}) copy-start(bf16[4,8,24,640]{3,2,0,1:T(8,128)(2,1)S(1)} %copy.94) | copy-start | bytes 2949124
  50.0 4.4 %collective-permute-start = (bf16[8,768]{1,0:T(8,128)(2,1)S(1)}, bf16[8,768]{1,0:T(8,128)(2,1)S(1)}, u32[]{:S(2)}, u32[]{:S(2)}) collective-permute-start(bf16[8,768]{1,0:T(8,128)(2,1)S(1)} %fusion.21), channel_id=1, source_target_pairs={{6,14},{7,15},{8,0},{9,1},{14,22},{15,23},{16,8},{17,9},{22,30},{2... | collective-permute-start | bytes 36872 | tf_op jit(solution)/shard_map/ppermute | solution.py:34
  55.2 9.6 %copy-start.17 = (s32[1,128]{1,0:T(1,128)S(1)}, s32[1,128]{1,0:T(1,128)}, u32[]{:S(2)}) copy-start(s32[1,128]{1,0:T(1,128)} %param.13) | copy-start | bytes 1540
  55.2 9.6 %copy-start.16 = (s32[1,128]{1,0:T(1,128)S(1)}, s32[1,128]{1,0:T(1,128)}, u32[]{:S(2)}) copy-start(s32[1,128]{1,0:T(1,128)} %param.14) | copy-start | bytes 1540
  55.2 9.8 %copy-start.15 = (bf16[1,128,367]{1,2,0:T(8,128)(2,1)S(1)}, bf16[1,128,367]{1,2,0:T(8,128)(2,1)}, u32[]{:S(2)}) copy-start(bf16[1,128,367]{1,2,0:T(8,128)(2,1)} %param.21) | copy-start | bytes 281860
  55.2 22.1 %copy-start.5 = (bf16[1,128,768]{2,1,0:T(8,128)(2,1)S(1)}, bf16[1,128,768]{2,1,0:T(8,128)(2,1)}, u32[]{:S(2)}) copy-start(bf16[1,128,768]{2,1,0:T(8,128)(2,1)} %param.12) | copy-start | bytes 589828
  56.6 20.8 %all-to-all-start.2 = ((bf16[8,64,384]{2,1,0:T(8,128)(2,1)}), bf16[8,64,384]{2,1,0:T(8,128)(2,1)S(1)}, u32[]{:S(2)}, u32[]{:S(2)}) async-start(bf16[8,64,384]{2,1,0:T(8,128)(2,1)} %bitcast.10), calls=%async_computation.2 | async-start | bytes 786432 | tf_op jit(solution)/shard_map/all_to_all | solution.py:365
  77.6 6.1 %collective-permute-start.1 = (bf16[128,768]{1,0:T(8,128)(2,1)S(1)}, bf16[128,768]{1,0:T(8,128)(2,1)S(1)}, u32[]{:S(2)}, u32[]{:S(2)}) collective-permute-start(bf16[128,768]{1,0:T(8,128)(2,1)S(1)} %get-tuple-element.37), channel_id=1, source_target_pairs={{0,8},{8,16},{16,24},{24,32},{32,40},{40,48},{48,56},{56,64},{64,7... | collective-permute-start | bytes 589832 | tf_op jit(solution)/shard_map/ppermute | solution.py:22
  80.5 7.1 %collective-permute-start.2 = (bf16[128,768]{1,0:T(8,128)(2,1)S(1)}, bf16[128,768]{1,0:T(8,128)(2,1)S(1)}, u32[]{:S(2)}, u32[]{:S(2)}) collective-permute-start(bf16[128,768]{1,0:T(8,128)(2,1)S(1)} %get-tuple-element.37), channel_id=1, source_target_pairs={{8,0},{16,8},{24,16},{32,24},{40,32},{48,40},{56,48},{64,56},{72,6... | collective-permute-start | bytes 589832 | tf_op jit(solution)/shard_map/ppermute | solution.py:22
  87.6 1.9 copy-start
  89.5 8.5 %copy-start.1 = (bf16[6144,256]{1,0:T(8,128)(2,1)S(1)}, bf16[6144,256]{1,0:T(8,128)(2,1)}, u32[]{:S(2)}) copy-start(bf16[6144,256]{1,0:T(8,128)(2,1)} %all-gather.7.cloned.1.call-done) | copy-start | bytes 9437188
  89.5 8.5 %copy-start.4 = (bf16[1,128,768]{2,1,0:T(8,128)(2,1)S(1)}, bf16[1,128,768]{2,1,0:T(8,128)(2,1)}, u32[]{:S(2)}) copy-start(bf16[1,128,768]{2,1,0:T(8,128)(2,1)} %param.20) | copy-start | bytes 589828
  90.9 13.9 %collective-permute-start.7 = (bf16[128,768]{1,0:T(8,128)(2,1)S(1)}, bf16[128,768]{1,0:T(8,128)(2,1)S(1)}, u32[]{:S(2)}, u32[]{:S(2)}) collective-permute-start(bf16[128,768]{1,0:T(8,128)(2,1)S(1)} %get-tuple-element.103), channel_id=1, source_target_pairs={{0,6},{2,0},{4,2},{6,4},{1,7},{3,1},{5,3},{7,5},{8,14},{10,8},{12,... | collective-permute-start | bytes 589832 | tf_op jit(solution)/shard_map/ppermute | solution.py:39
  92.4 12.4 %collective-permute-start.6 = (bf16[128,768]{1,0:T(8,128)(2,1)S(1)}, bf16[128,768]{1,0:T(8,128)(2,1)S(1)}, u32[]{:S(2)}, u32[]{:S(2)}) collective-permute-start(bf16[128,768]{1,0:T(8,128)(2,1)S(1)} %get-tuple-element.104), channel_id=1, source_target_pairs={{0,4},{2,6},{4,0},{6,2},{1,5},{3,7},{5,1},{7,3},{8,12},{10,14},{12... | collective-permute-start | bytes 589832 | tf_op jit(solution)/shard_map/ppermute | solution.py:39
  93.1 11.7 %collective-permute-start.5 = (bf16[128,768]{1,0:T(8,128)(2,1)S(1)}, bf16[128,768]{1,0:T(8,128)(2,1)S(1)}, u32[]{:S(2)}, u32[]{:S(2)}) collective-permute-start(bf16[128,768]{1,0:T(8,128)(2,1)S(1)} %get-tuple-element.105), channel_id=1, source_target_pairs={{0,2},{2,4},{4,6},{6,0},{1,3},{3,5},{5,7},{7,1},{8,10},{10,12},{12... | collective-permute-start | bytes 589832 | tf_op jit(solution)/shard_map/ppermute | solution.py:39
  93.1 5.6 %collective-permute-start.3 = (bf16[80,768]{1,0:T(8,128)(2,1)S(1)}, bf16[80,768]{1,0:T(8,128)(2,1)S(1)}, u32[]{:S(2)}, u32[]{:S(2)}) collective-permute-start(bf16[80,768]{1,0:T(8,128)(2,1)S(1)} %get-tuple-element.43), channel_id=1, source_target_pairs={{0,8},{8,16},{16,24},{24,32},{32,40},{40,48},{48,56},{56,64},{64,7... | collective-permute-start | bytes 368648 | tf_op jit(solution)/shard_map/ppermute | solution.py:22
  96.7 6.1 %collective-permute-start.4 = (bf16[80,768]{1,0:T(8,128)(2,1)S(1)}, bf16[80,768]{1,0:T(8,128)(2,1)S(1)}, u32[]{:S(2)}, u32[]{:S(2)}) collective-permute-start(bf16[80,768]{1,0:T(8,128)(2,1)S(1)} %get-tuple-element.44), channel_id=1, source_target_pairs={{8,0},{16,8},{24,16},{32,24},{40,32},{48,40},{56,48},{64,56},{72,6... | collective-permute-start | bytes 368648 | tf_op jit(solution)/shard_map/ppermute | solution.py:22
  98.7 6.1 %copy-start.7 = (bf16[128,367]{1,0:T(8,128)(2,1)}, bf16[128,367]{1,0:T(8,128)(2,1)S(1)}, u32[]{:S(2)}) copy-start(bf16[128,367]{1,0:T(8,128)(2,1)S(1)} %get-tuple-element.40) | copy-start | bytes 281860
  104.9 21.9 %all-to-all-start.3 = ((bf16[8,64,896]{2,1,0:T(8,128)(2,1)}), bf16[8,64,896]{2,1,0:T(8,128)(2,1)S(1)}, u32[]{:S(2)}, u32[]{:S(2)}) async-start(bf16[8,64,896]{2,1,0:T(8,128)(2,1)} %get-tuple-element.49), calls=%async_computation.3 | async-start | bytes 1835008 | tf_op jit(solution)/shard_map/all_to_all | solution.py:405
  113.1 59.9 %reduce-scatter.2.cloned.1.call-start = ((), (), s32[]{:S(2)}) async-start(), calls=%async_computation.8 | async-start | bytes 884736 | tf_op jit(solution)/shard_map/reduce_scatter | solution.py:421
  113.1 19.2 %collective-permute-start.8 = (bf16[4,128,768]{2,1,0:T(8,128)(2,1)S(1)}, bf16[4,128,768]{2,1,0:T(8,128)(2,1)S(1)}, u32[]{:S(2)}, u32[]{:S(2)}) collective-permute-start(bf16[4,128,768]{2,1,0:T(8,128)(2,1)S(1)} %pad_maximum_fusion.near_ref), channel_id=1, source_target_pairs={{0,1},{1,0},{2,3},{3,2},{4,5},{5,4},{6,7},{7,6},{8,9},{9,8},{10,11... | collective-permute-start | bytes 2359304 | tf_op jit(solution)/shard_map/ppermute | solution.py:43
  126.9 9.3 %collective-permute-start.9 = (bf16[8,384]{1,0:T(8,128)(2,1)S(1)}, bf16[8,384]{1,0:T(8,128)(2,1)S(1)}, u32[]{:S(2)}, u32[]{:S(2)}) collective-permute-start(bf16[8,384]{1,0:T(8,128)(2,1)S(1)} %bitcast.57), channel_id=1, source_target_pairs={{0,8},{1,9},{8,16},{9,17},{14,6},{15,7},{16,24},{17,25},{22,14},{2... | collective-permute-start | bytes 18440 | tf_op jit(solution)/shard_map/ppermute | solution.py:34
  132.4 0.9 copy-start.2
  133.2 1.1 copy-start.3
  134.4 2.2 %copy-start.14 = (bf16[4,8,24,640]{3,2,0,1:T(8,128)(2,1)S(1)}, bf16[4,8,24,640]{3,2,0,1:T(8,128)(2,1)}, u32[]{:S(2)}) copy-start(bf16[4,8,24,640]{3,2,0,1:T(8,128)(2,1)} %copy-done.13) | copy-start | bytes 2949124
  156.0 25.5 %copy-start.8 = (bf16[128,367]{1,0:T(8,128)(2,1)S(1)}, bf16[128,367]{1,0:T(8,128)(2,1)}, u32[]{:S(2)}) copy-start(bf16[128,367]{1,0:T(8,128)(2,1)} %copy-done.7) | copy-start | bytes 281860
  173.8 14.1 %all-to-all-start.6 = ((bf16[8,24,640]{2,1,0:T(8,128)(2,1)}), bf16[8,24,640]{2,1,0:T(8,128)(2,1)S(1)}, u32[]{:S(2)}, u32[]{:S(2)}) async-start(bf16[8,24,640]{2,1,0:T(8,128)(2,1)} %broadcast_in_dim.44), calls=%async_computation.7 | async-start | bytes 491520 | tf_op jit(solution)/shard_map/all_to_all | solution.py:428
  (2 other events, 1.5 us)
Sparse Core Ops, SparseCore 0:
  13.5 30.3 all-gather.4
  49.1 33.3 all-gather.6
  138.2 34.7 reduce-scatter.1

commit v2 on v1

--- a/solution.py
+++ b/solution.py
@@ -55,16 +55,15 @@
     return lax.dot_general(left, right, (((0,), (0,)), ((), ())), preferred_element_type=F32)
 
 
-def call(body, shapes, *operands, scratch=(), scalars=0):
+def call(body, shapes, *operands, scratch=(), mib=16):
     vmem = pl.BlockSpec(memory_space=pltpu.VMEM)
-    smem = pl.BlockSpec(memory_space=pltpu.SMEM)
     return pl.pallas_call(
         body,
         out_shape=[jax.ShapeDtypeStruct(shape, kind) for shape, kind in shapes],
-        in_specs=[smem] * scalars + [vmem] * (len(operands) - scalars),
+        in_specs=[vmem] * len(operands),
         out_specs=[vmem] * len(shapes),
-        scratch_shapes=[pltpu.VMEM(shape, kind) for shape, kind in scratch],
-        compiler_params=pltpu.CompilerParams(vmem_limit_bytes=16 * 1024 * 1024),
+        scratch_shapes=list(scratch),
+        compiler_params=pltpu.CompilerParams(vmem_limit_bytes=mib * 1024 * 1024),
     )(*operands)
 
 
@@ -82,28 +81,70 @@
 
 
 def start_body(
-    place_ref, conv_ref, donor_ref, acceptor_ref, track_ref, gain_ref, coarse_ref, out_ref, own_ref
+    conv_ref, donor_ref, acceptor_ref, track_ref, gain_ref, coarse_ref, out_ref, own_ref
 ):
-    x, c = place_ref[0], place_ref[1]
-    half = out_ref.shape[1] - CHUNK
+    x, c = lax.axis_index("x"), lax.axis_index("c")
+    half = out_ref.shape[2] - CHUNK
     half_rows = coarse_ref.shape[0]
     own_ref[:half_rows] = coarse_ref[...]
     own_ref[half_rows:] = jnp.zeros_like(own_ref[half_rows:])
-    depth = out_ref.shape[0]
+    copies, depth = out_ref.shape[:2]
     for member in range(8):
         tap, part = member // 2, member % 2
 
         @pl.when((x == tap) & (c == part))
         def _():
-            out_ref[:, :half] = conv_ref[:, tap, part * half : (part + 1) * half]
+            taps = conv_ref[:, tap, part * half : (part + 1) * half]
             if member == 7:
                 tracks = track_ref.shape[1]
                 pad = jnp.zeros((depth, 2 * CHUNK - tracks - 1), BF)
-                out_ref[:, half:] = jnp.concatenate([track_ref[:, CHUNK:], gain_ref[...], pad], 1)
+                row = lax.broadcasted_iota(jnp.int32, (depth, depth), 0)
+                lane = lax.broadcasted_iota(jnp.int32, (depth, depth), 1)
+                gains = jnp.where(row == lane, gain_ref[...].astype(F32), 0.0)
+                gains = jnp.sum(gains, 1, keepdims=True).astype(BF)
+                rest = jnp.concatenate([track_ref[:, CHUNK:], gains, pad], 1)
             else:
                 source = (donor_ref, acceptor_ref, track_ref)[member // 3]
                 first = (member % 3) * CHUNK
-                out_ref[:, half:] = source[:, first : first + CHUNK]
+                rest = source[:, first : first + CHUNK]
+            for index in range(copies):
+                out_ref[index, :, :half] = taps
+                out_ref[index, :, half:] = rest
+
+
+def shift_rows(x, down, up, load, edge_ref, rows_ref, members):
+    depth = rows_ref.shape[0] // members
+    for member in range(members):
+        span = slice(member * depth, (member + 1) * depth)
+
+        @pl.when(x == up)
+        def _():
+            block = load(member).astype(F32)
+            edge = edge_ref[member : member + 1].astype(F32)
+            rows_ref[span] = jnp.concatenate([block[1:], edge], 0).astype(BF)
+
+        @pl.when(x == down)
+        def _():
+            block = load(member).astype(F32)
+            edge = edge_ref[member : member + 1].astype(F32)
+            rows_ref[span] = jnp.concatenate([edge, block[:-1]], 0).astype(BF)
+
+        @pl.when((x != down) & (x != up))
+        def _():
+            rows_ref[span] = load(member)
+
+
+def conv_body(both_ref, left_ref, edge_ref, out_ref, weight_ref, rows_ref):
+    x = lax.axis_index("x")
+    wide_y, wide_z, _, _ = both_ref.shape
+    members, half_rows, half = out_ref.shape
+    planes = [
+        both_ref[y, z, :, :half].astype(F32) for z in range(wide_z) for y in range(wide_y)
+    ]
+    weight_ref[...] = jnp.concatenate(planes, 0).astype(BF)
+    shift_rows(x, 3, 0, lambda member: left_ref[member, :half_rows], edge_ref, rows_ref, members)
+    result = mm(rows_ref[...], weight_ref[...]).astype(BF)
+    out_ref[...] = result.reshape(members, half_rows, half)
 
 
 def norm_body(taps_ref, skip_ref, pre_ref, unit_ref):
@@ -186,9 +227,9 @@
 def base_body(product_ref, chunks_ref, place_ref, fine_ref, scores_ref, base_ref):
     rows = fine_ref.shape[0]
     product = product_ref[...]
-    tracks = scores_ref.shape[1]
-    scores_ref[:, :CHUNK] = mm(product, chunks_ref[6]).astype(BF)
-    scores_ref[:, CHUNK:] = mm(product, chunks_ref[7])[:, : tracks - CHUNK].astype(BF)
+    tracks = scores_ref.shape[0]
+    scores_ref[:CHUNK] = mm(product, chunks_ref[6]).T.astype(BF)
+    scores_ref[CHUNK:] = mm(product, chunks_ref[7]).T[: tracks - CHUNK].astype(BF)
     place = place_ref[...]
     total = mm(split_hot(rows, True), fine_ref[...])
     for index in range(3):
@@ -245,8 +286,8 @@
     out_ref[7, :, half + 128 : half + CHUNK] = gain_block.astype(BF)
 
 
-def partial_body(place_ref, left_ref, near_ref, far_ref, grads_ref, out_ref, rows_ref, right_ref):
-    x, c = place_ref[0], place_ref[1]
+def partial_body(left_ref, near_ref, far_ref, grads_ref, out_ref, rows_ref, right_ref):
+    x, c = lax.axis_index("x"), lax.axis_index("c")
     members, half_rows, _ = grads_ref.shape
     half = left_ref.shape[1] // 2
     rows = 2 * half_rows
@@ -291,20 +332,62 @@
     )
 
 
-def final_body(rescale, shares_ref, conv_ref, donor_ref, acceptor_ref, track_ref, gain_ref):
+def back_body(grads_ref, edge_ref, weight_ref, mine_ref, other_ref, rows_ref):
+    x, c = lax.axis_index("x"), lax.axis_index("c")
+    members, half_rows, _ = grads_ref.shape
+    half = weight_ref.shape[1]
+    shift_rows(x, 0, 3, lambda member: grads_ref[member, :, :half], edge_ref, rows_ref, members)
+    result = mm_nt(rows_ref[...], weight_ref[...]).astype(BF)
+    for member in range(members):
+        block = result[member * half_rows : (member + 1) * half_rows]
+        step = lax.rem(member // 2 - x + 4, 4)
+
+        @pl.when(c == member % 2)
+        def _():
+            mine_ref[step] = block
+
+        @pl.when(c != member % 2)
+        def _():
+            other_ref[step] = block
+
+
+def add_body(left_ref, right_ref, out_ref):
+    out_ref[...] = (left_ref[...].astype(F32) + right_ref[...].astype(F32)).astype(BF)
+
+
+def copies_body(parts_ref, out_ref):
+    total = parts_ref[0].astype(F32)
+    for index in range(1, parts_ref.shape[0]):
+        total = total + parts_ref[index].astype(F32)
+    total = total.astype(BF)
+    for index in range(out_ref.shape[0]):
+        out_ref[index] = total
+
+
+def final_body(
+    rescale, shares_ref, backs_ref, conv_ref, donor_ref, acceptor_ref, track_ref, gain_ref, back_ref
+):
     half = conv_ref.shape[2] // 2
     tracks = track_ref.shape[1]
+    back = backs_ref[0].astype(F32)
+    for member in range(1, backs_ref.shape[0]):
+        back = back + backs_ref[member].astype(F32)
+    back_ref[...] = back.astype(BF)
     for member in range(8):
         values = shares_ref[member].astype(F32) * rescale
         tap, part = member // 2, member % 2
         conv_ref[:, tap, part * half : (part + 1) * half] = values[:, :half]
         if member == 7:
             track_ref[:, CHUNK:] = values[:, half : half + tracks - CHUNK]
-            gain_ref[...] = values[:, half + CHUNK // 2 : half + CHUNK // 2 + 1]
+            depth = values.shape[0]
+            column = values[:, half + CHUNK // 2 : half + CHUNK // 2 + 1]
+            row = lax.broadcasted_iota(jnp.int32, (depth, depth), 0)
+            lane = lax.broadcasted_iota(jnp.int32, (depth, depth), 1)
+            gain_ref[...] = jnp.sum(jnp.where(row == lane, column, 0.0), 0, keepdims=True)
         else:
             target = (donor_ref, acceptor_ref, track_ref)[member // 3]
             first = (member % 3) * CHUNK
-            target[:, first : first + CHUNK] = values[:, half:]
+            target[:, first : first + CHUNK] = values[:, half : half + CHUNK]
 
 
 def local(
@@ -334,34 +417,29 @@
     batch = lax.axis_index(GROUP)
     x, c = lax.axis_index("x"), lax.axis_index("c")
 
-    place = jnp.stack([x, c])
     both, own = call(
         start_body,
-        [((rows_in, half + CHUNK), BF), ((half_rows + 32, channels), BF)],
-        place, conv_weight, donor_weight, acceptor_weight, track_weight, gain[:, None], coarse[0],
-        scalars=1,
-    )
-    both = jnp.broadcast_to(both[None], (nz, rows_in, half + CHUNK))
+        [((nz, rows_in, half + CHUNK), BF), ((half_rows + 32, channels), BF)],
+        conv_weight, donor_weight, acceptor_weight, track_weight, gain[None, :], coarse[0],
+        mib=56,
+    )
     both = lax.all_to_all(both, "z", 0, 0, tiled=True)
 
-    def over_y(block):
-        block = jnp.broadcast_to(block[None], (ny,) + block.shape)
-        block = lax.all_to_all(block, "y", 0, 0, tiled=True)
-        return jnp.swapaxes(block, 0, 1).reshape(channels, block.shape[-1])
-
-    gathered = over_y(both)
-    conv_w = gathered[:, :half]
-    chunks = lax.all_gather(gathered[:, half:], GROUP, axis=0)
-
-    left_all = lax.all_gather(own, GROUP, axis=0)[:, :half_rows]
+    both = jnp.broadcast_to(both[None], (ny,) + both.shape)
+    both = lax.all_to_all(both, "y", 0, 0, tiled=True)
+    rest_mine = jnp.swapaxes(both[:, :, :, half:], 0, 1).reshape(channels, CHUNK)
+
+    left_all = lax.all_gather(own, GROUP, axis=0)
     edge = jnp.where(x == 0, left_all[:, 0], left_all[:, half_rows - 1])
-    edge = send_edge(edge, (-1, 0, 0, 1))[:, None]
-    wide_rows = jnp.concatenate([edge, left_all, edge], 1)
-    first_row = jnp.where(x == 0, 2, jnp.where(x == nx - 1, 0, 1))
-    left_rows = lax.dynamic_slice_in_dim(wide_rows, first_row, half_rows, 1)
-    left_rows = left_rows.reshape(-1, channels)
-
-    tap_out = mm(left_rows, conv_w).astype(BF).reshape(group_size, half_rows, half)
+    edge = send_edge(edge, (-1, 0, 0, 1))
+    tap_out, conv_w, left_rows = call(
+        conv_body,
+        [((group_size, half_rows, half), BF), ((channels, half), BF)]
+        + [((group_size * half_rows, channels), BF)],
+        both, left_all, edge,
+    )
+    rest_mine, tap_out = lax.optimization_barrier((rest_mine, tap_out))
+    chunks = lax.all_gather(rest_mine, GROUP, axis=0)
     taps = lax.all_to_all(tap_out, GROUP, 0, 0, tiled=True)
 
     def split_place(place):
@@ -383,7 +461,7 @@
         + [(fine_shape, F32), ((16, channels), F32)],
         pre_norm, chunks, near_low, near_high, donor_place, acceptor_place, group[:, None], group[None, :],
         score_grad[0],
-        scratch=[(fine_shape, BF), (fine_shape, BF)],
+        scratch=[pltpu.VMEM(fine_shape, BF), pltpu.VMEM(fine_shape, BF)],
     )
     grads_high = send_seq(to_low, -1)
     grads_low = send_seq(to_high, 1)
@@ -393,7 +471,7 @@
         left_near[:1] + [send_x(left_near[step], step) for step in range(1, nx)], 0
     )
     scores, base = call(
-        base_body, [((pairs, tracks), BF), (fine_shape, F32)], product, chunks, place_donor, fine_grad[0]
+        base_body, [((tracks, pairs), BF), (fine_shape, F32)], product, chunks, place_donor, fine_grad[0]
     )
     skip_out, outgoing = call(
         skip_body,
@@ -405,39 +483,43 @@
     grads = lax.all_to_all(outgoing, GROUP, 0, 0, tiled=True)
     tap_grads = grads[:, :, :half]
     grad_edge = jnp.where(x == 0, tap_grads[:, half_rows - 1], tap_grads[:, 0])
-    grad_edge = send_edge(grad_edge, (1, 0, 0, -1))[:, None]
+    grad_edge = send_edge(grad_edge, (1, 0, 0, -1))
     (partials,) = call(
         partial_body,
         [((ny, nz, rows_in, half + CHUNK), BF)],
-        place, left_rows, left_near, left_far, grads,
-        scratch=[((group_size * fine_rows, channels), BF), ((group_size * fine_rows, CHUNK), BF)],
-        scalars=1,
-    )
-    wide_grads = jnp.concatenate([grad_edge, tap_grads, grad_edge], 1)
-    first_grad = jnp.where(x == 0, 0, jnp.where(x == nx - 1, 2, 1))
-    moved = lax.dynamic_slice_in_dim(wide_grads, first_grad, half_rows, 1).reshape(-1, half)
-    back = mm_nt(moved, conv_w).astype(BF).reshape(group_size, half_rows, channels)
-    partials, back = lax.optimization_barrier((partials, back))
-    coarse_back = lax.psum_scatter(back, GROUP, scatter_dimension=0, tiled=True)
+        left_rows, left_near, left_far, grads,
+        scratch=[
+            pltpu.VMEM((group_size * fine_rows, channels), BF),
+            pltpu.VMEM((group_size * fine_rows, CHUNK), BF),
+        ],
+    )
+    slabs = (nx, half_rows, channels)
+    back_mine, back_other = call(
+        back_body, [(slabs, BF), (slabs, BF)], grads, grad_edge, conv_w,
+        scratch=[pltpu.VMEM((group_size * half_rows, half), BF)],
+    )
+    (back_sum,) = call(add_body, [(slabs, BF)], back_mine, swap_core(back_other))
+    backs = jnp.stack(
+        [back_sum[0]] + [send_x(back_sum[step], step) for step in range(1, nx)], 0
+    )
     shares = lax.all_to_all(partials, "y", 0, 0, tiled=True)
     shares = jnp.sum(shares.astype(F32), 0).astype(BF)
     shares = lax.all_to_all(shares, "z", 0, 0, tiled=True)
-    shares, coarse_back = lax.optimization_barrier((shares, coarse_back))
-    shares = jnp.sum(shares.astype(F32), 0).astype(BF)
-    shares = jnp.broadcast_to(shares[None], (group_size,) + shares.shape)
+    shares, backs = lax.optimization_barrier((shares, backs))
+    (shares,) = call(copies_body, [((group_size, rows_in, half + CHUNK), BF)], shares)
     shares = lax.all_to_all(shares, GROUP, 0, 0, tiled=True)
 
     rescale = float(group_size * seqs * fine_rows) ** (-0.5)
-    conv_grad, donor_grad, acceptor_grad, track_grad, gain_grad = call(
+    conv_grad, donor_grad, acceptor_grad, track_grad, gain_grad, coarse_back = call(
         functools.partial(final_body, rescale),
         [((rows_in, nx, channels), F32), ((rows_in, channels), F32), ((rows_in, channels), F32)]
-        + [((rows_in, tracks), F32), ((rows_in, 1), F32)],
-        shares,
-    )
-    gain_grad = gain_grad[:, 0]
+        + [((rows_in, tracks), F32), ((1, rows_in), F32), ((half_rows, channels), BF)],
+        shares, backs,
+    )
+    gain_grad = gain_grad[0]
     return (
-        scores[None],
-        coarse_back,
+        scores.T[None],
+        coarse_back[None],
         skip_out[None],
         conv_grad,
         donor_grad,

time: 197 us -> 181 us (0.919)
  blocking collectives: 68.5 us -> 31.3 us
  waiting for transfers between devices: 43.6 us -> 62.3 us
  starting transfers between devices: 42.3 us -> 50.7 us
  local copies, waits for them, and re-layouts: 13.8 us -> 8 us
  Pallas kernels: 8.22 us -> 11.8 us
  matrix products: 2.83 us -> 0 us
    all_to_all x3 -> x1, blocking collectives: 49.7 us -> 12.3 us  [local(): shares = lax.all_to_all(shares, GROUP, 0, 0, tiled=True)]
    all_gather x2, waiting for transfers between devices: 0.02 us -> 14.5 us  [the longest x1 7.47 us: local(): left_all = lax.all_gather(own, GROUP, axis=0)]
    all_to_all x1 -> x3, starting transfers between devices: 7.74 us -> 17 us  [the longest x1 6.95 us: local(): shares = lax.all_to_all(shares, 'z', 0, 0, tiled=True)]
    ppermute x3 -> x6, waiting for transfers between devices: 0.01 us -> 7.49 us  [send_x(): lax.ppermute(block, 'x', [(i, (i + step) % count) for i in range(count)])]
    ppermute x2, waiting for transfers between devices: 1.92 us -> 7.93 us  [send_edge(): return lax.ppermute(block, AXES, pairs)]
    all_to_all x1, waiting for transfers between devices: 11.9 us -> 7.45 us  [local(): taps = lax.all_to_all(tap_out, GROUP, 0, 0, tiled=True)]
    all_to_all x1 -> x3, waiting for transfers between devices: 5.6 us -> 1.49 us  [the longest x1 1.49 us: local(): both = lax.all_to_all(both, 'y', 0, 0, tiled=True)]
    unnamed x39 -> x23, local copies, waits for them, and re-layouts: 8.89 us -> 4.79 us
  transfers between devices with their start and end apart: 16 -> 21, of which waited for: 8 -> 16; matrix products, arithmetic and copies ran while one was open for 3% -> 2% of each run, Pallas kernels for 2% -> 3%
where the time goes in v2:
time: 181 us; the launch traced here: 180 us
  waiting for transfers between devices  62.3 us (34%)
  starting transfers between devices  50.7 us (28%)
  blocking collectives  31.3 us (17%)
  between operations  14.3 us (8%)
  Pallas kernels  11.8 us (7%)
  local copies, waits for them, and re-layouts  8 us (4%)
    all_to_all x1, blocking collectives, local(): both = lax.all_to_all(both, 'z', 0, 0, tiled=True)  19 us
    all_to_all x1, blocking collectives, local(): shares = lax.all_to_all(shares, GROUP, 0, 0, tiled=True)  12.3 us
    pallas_call x11, Pallas kernels, call(): pl.pallas_call(body, out_shape=[jax.ShapeDtypeStruct(shape, kind) for sha...  11.8 us
    all_to_all x1, waiting for transfers between devices, local(): grads = lax.all_to_all(outgoing, GROUP, 0, 0, tiled=True)  10.5 us
    ppermute x4, waiting for transfers between devices, send_seq(): return lax.ppermute(block, SEQ, pairs)  9.28 us
    ppermute x2, waiting for transfers between devices, send_edge(): return lax.ppermute(block, AXES, pairs)  7.93 us
    ppermute x4, starting transfers between devices, send_seq(): return lax.ppermute(block, SEQ, pairs)  7.85 us
    ppermute x6, waiting for transfers between devices, send_x(): lax.ppermute(block, 'x', [(i, (i + step) % count) for i in range(count)])  7.49 us
  transfers between devices with their start and end apart: 21, of which 16 were waited for; matrix products, arithmetic and copies ran while one was open for 2% of the time, Pallas kernels for 3%

profile of v2, /device:TPU:1, one launch (start us, length us, event | category | flops | bytes accessed | tf_op | source)
XLA Modules:
  0.0 179.7 jit_solution(4203776754767438525)
XLA Ops:
  7.2 1.9 %shard_map.170 = (bf16[8,24,640]{2,1,0:T(8,128)(2,1)}, bf16[96,768]{1,0:T(8,128)(2,1)}) custom-call(bf16[24,4,768]{2,1,0:T(4,128)(2,1)} %conv_ref.1, bf16[24,768]{1,0:T(8,128)(2,1)} %donor_ref.1, bf16[24,768]{1,0:T(8,128)(2,1)} %acceptor_ref.1, bf16[24,367]{1,0:T(8,128)(2,1)} %track_ref.1, bf16[1,24]{1,0:T(2,128)(2,1)} %bitcast.54, bf16[64,768]{1,0:T(8,128)(2,1)} %bitcast.53), custom_call_target="tpu_custom_call" | custom-call | tf_op jit(solution)/shard_map/pallas_call | solution.py:60
  9.1 19.0 %all_to_all.35 = bf16[8,24,640]{2,1,0:T(8,128)(2,1)S(1)} all-to-all(bf16[8,24,640]{2,1,0:T(8,128)(2,1)} %get-tuple-element.40), channel_id=1, replica_groups=mesh['z'=8,'y'=4,'x'=4,'c'=2] {'z'}, dimensions={0} | all-to-all | bytes 491520 | tf_op jit(solution)/shard_map/all_to_all | solution.py:426
  29.2 4.2 %all-to-all-start.1 = ((bf16[4,8,24,640]{3,2,1,0:T(8,128)(2,1)}), bf16[4,8,24,640]{3,2,1,0:T(8,128)(2,1)S(1)}, u32[]{:S(2)}, u32[]{:S(2)}) async-start(bf16[4,8,24,640]{3,2,1,0:T(8,128)(2,1)} %broadcast_in_dim.11), calls=%async_computation.1 | async-start | bytes 1966080 | tf_op jit(solution)/shard_map/all_to_all | solution.py:429
  33.4 7.5 %all-gather.5.cloned.1.call-done = bf16[768,768]{1,0:T(8,128)(2,1)} async-done(((bf16[96,768]{1,0:T(8,128)(2,1)}), bf16[768,768]{1,0:T(8,128)(2,1)}) %all-gather.5.cloned.1.call-update) | async-done | bytes 1179664 | tf_op jit(solution)/shard_map/all_gather | solution.py:432
  43.2 1.5 all-to-all-done.1.both_ref
  48.5 7.0 %all-to-all-start.2 = ((bf16[8,64,384]{2,1,0:T(8,128)(2,1)}), bf16[8,64,384]{2,1,0:T(8,128)(2,1)S(1)}, u32[]{:S(2)}, u32[]{:S(2)}) async-start(bf16[8,64,384]{2,1,0:T(8,128)(2,1)} %copy-done.5), calls=%async_computation.2 | async-start | bytes 786432 | tf_op jit(solution)/shard_map/all_to_all | solution.py:443
  56.2 7.5 %all-to-all-done.2.taps_ref = bf16[8,64,384]{2,1,0:T(8,128)(2,1)S(1)} async-done(((bf16[8,64,384]{2,1,0:T(8,128)(2,1)}), bf16[8,64,384]{2,1,0:T(8,128)(2,1)S(1)}, u32[]{:S(2)}, u32[]{:S(2)}) %all-to-all-start.2) | async-done | bytes 393248 | tf_op jit(solution)/shard_map/all_to_all | solution.py:443
  63.9 2.2 %collective-permute-start.1 = (bf16[128,768]{1,0:T(8,128)(2,1)S(1)}, bf16[128,768]{1,0:T(8,128)(2,1)S(1)}, u32[]{:S(2)}, u32[]{:S(2)}) collective-permute-start(bf16[128,768]{1,0:T(8,128)(2,1)S(1)} %get-tuple-element.46), channel_id=1, source_target_pairs={{0,8},{8,16},{16,24},{24,32},{32,40},{40,48},{48,56},{56,64},{64,7... | collective-permute-start | bytes 589832 | tf_op jit(solution)/shard_map/ppermute | solution.py:22
  67.4 2.0 %collective-permute-done.1.low_ref = bf16[128,768]{1,0:T(8,128)(2,1)S(1)} collective-permute-done((bf16[128,768]{1,0:T(8,128)(2,1)S(1)}, bf16[128,768]{1,0:T(8,128)(2,1)S(1)}, u32[]{:S(2)}, u32[]{:S(2)}) %collective-permute-start.1) | collective-permute-done | bytes 196640 | tf_op jit(solution)/shard_map/ppermute | solution.py:22
  69.4 3.9 %collective-permute-done.2.high_ref = bf16[128,768]{1,0:T(8,128)(2,1)S(1)} collective-permute-done((bf16[128,768]{1,0:T(8,128)(2,1)S(1)}, bf16[128,768]{1,0:T(8,128)(2,1)S(1)}, u32[]{:S(2)}, u32[]{:S(2)}) %collective-permute-start.2) | collective-permute-done | bytes 196640 | tf_op jit(solution)/shard_map/ppermute | solution.py:22
  73.3 7.0 %all-gather.7.cloned.1.call-done = bf16[6144,256]{1,0:T(8,128)(2,1)} async-done(((bf16[768,256]{1,0:T(8,128)(2,1)}), bf16[6144,256]{1,0:T(8,128)(2,1)}) %all-gather.7.cloned.1.call-update) | async-done | bytes 3145744 | tf_op jit(solution)/shard_map/all_gather | solution.py:442
  80.3 1.9 %copy-done = bf16[6144,256]{1,0:T(8,128)(2,1)S(1)} copy-done((bf16[6144,256]{1,0:T(8,128)(2,1)S(1)}, bf16[6144,256]{1,0:T(8,128)(2,1)}, u32[]{:S(2)}) %copy-start) | copy-done | bytes 3145752
  82.2 1.4 shard_map.173
  83.7 1.4 collective-permute-start.7
  86.1 3.1 %collective-permute-start.3 = (bf16[80,768]{1,0:T(8,128)(2,1)S(1)}, bf16[80,768]{1,0:T(8,128)(2,1)S(1)}, u32[]{:S(2)}, u32[]{:S(2)}) collective-permute-start(bf16[80,768]{1,0:T(8,128)(2,1)S(1)} %get-tuple-element.53), channel_id=1, source_target_pairs={{0,8},{8,16},{16,24},{24,32},{32,40},{40,48},{48,56},{56,64},{64,7... | collective-permute-start | bytes 368648 | tf_op jit(solution)/shard_map/ppermute | solution.py:22
  91.7 3.4 %collective-permute-done.4.high_ref = bf16[80,768]{1,0:T(8,128)(2,1)S(1)} collective-permute-done((bf16[80,768]{1,0:T(8,128)(2,1)S(1)}, bf16[80,768]{1,0:T(8,128)(2,1)S(1)}, u32[]{:S(2)}, u32[]{:S(2)}) %collective-permute-start.4) | collective-permute-done | bytes 122912 | tf_op jit(solution)/shard_map/ppermute | solution.py:22
  95.1 2.0 %shard_map.175 = (bf16[128,768]{1,0:T(8,128)(2,1)}, bf16[8,64,896]{2,1,0:T(8,128)(2,1)}) custom-call(f32[128,768]{1,0:T(8,128)S(1)} %get-tuple-element.51.base_ref, f32[128,768]{1,0:T(8,128)S(1)} %get-tuple-element.52.own_ref, bf16[8,768,256]{2,1,0:T(8,128)(2,1)S(1)} %bitcast.39, bf16[80,768]{1,0:T(8,128)(2,1)S(1)} %collective-permute-done.3.low_ref, ...), custom_call_target="tpu_custom_call" | custom-call | tf_op jit(solution)/shard_map/pallas_call | solution.py:60
  97.7 6.1 %all-to-all-start.3 = ((bf16[8,64,896]{2,1,0:T(8,128)(2,1)}), bf16[8,64,896]{2,1,0:T(8,128)(2,1)S(1)}, u32[]{:S(2)}, u32[]{:S(2)}) async-start(bf16[8,64,896]{2,1,0:T(8,128)(2,1)} %get-tuple-element.59), calls=%async_computation.3 | async-start | bytes 1835008 | tf_op jit(solution)/shard_map/all_to_all | solution.py:483
  103.8 2.3 %collective-permute-done.8.far_ref = bf16[4,128,768]{2,1,0:T(8,128)(2,1)S(1)} collective-permute-done((bf16[4,128,768]{2,1,0:T(8,128)(2,1)S(1)}, bf16[4,128,768]{2,1,0:T(8,128)(2,1)S(1)}, u32[]{:S(2)}, u32[]{:S(2)}) %collective-permute-start.8) | collective-permute-done | bytes 786464 | tf_op jit(solution)/shard_map/ppermute | solution.py:43
  106.9 10.5 %all-to-all-done.3.grads_ref = bf16[8,64,896]{2,1,0:T(8,128)(2,1)S(1)} async-done(((bf16[8,64,896]{2,1,0:T(8,128)(2,1)}), bf16[8,64,896]{2,1,0:T(8,128)(2,1)S(1)}, u32[]{:S(2)}, u32[]{:S(2)}) %all-to-all-start.3) | async-done | bytes 917536 | tf_op jit(solution)/shard_map/all_to_all | solution.py:483
  118.6 2.2 %shard_map.176 = bf16[4,8,24,640]{3,2,1,0:T(8,128)(2,1)} custom-call(bf16[512,768]{1,0:T(8,128)(2,1)S(1)} %get-tuple-element.50.left_ref, bf16[4,128,768]{2,1,0:T(8,128)(2,1)S(1)} %pad_maximum_fusion.near_ref, bf16[4,128,768]{2,1,0:T(8,128)(2,1)S(1)} %copy-done.4, bf16[8,64,896]{2,1,0:T(8,128)(2,1)S(1)} %all-to-all-done.3.grads_ref), custom_call_target="tpu_custom_call" | custom-call | tf_op jit(solution)/shard_map/pallas_call | solution.py:60
  120.8 5.8 %all-to-all-start.4 = ((bf16[4,8,24,640]{3,2,1,0:T(8,128)(2,1)}), bf16[4,8,24,640]{3,2,1,0:T(8,128)(2,1)S(1)}, u32[]{:S(2)}, u32[]{:S(2)}) async-start(bf16[4,8,24,640]{3,2,1,0:T(8,128)(2,1)} %shard_map.176), calls=%async_computation.4 | async-start | bytes 1966080 | tf_op jit(solution)/shard_map/all_to_all | solution.py:505
  126.7 3.4 %collective-permute-start.9 = (bf16[8,384]{1,0:T(8,128)(2,1)S(1)}, bf16[8,384]{1,0:T(8,128)(2,1)S(1)}, u32[]{:S(2)}, u32[]{:S(2)}) collective-permute-start(bf16[8,384]{1,0:T(8,128)(2,1)S(1)} %fusion.16), channel_id=1, source_target_pairs={{0,8},{1,9},{8,16},{9,17},{14,6},{15,7},{16,24},{17,25},{22,14},{2... | collective-permute-start | bytes 18440 | tf_op jit(solution)/shard_map/ppermute | solution.py:34
  130.0 6.6 %collective-permute-done.9.edge_ref = bf16[8,384]{1,0:T(8,128)(2,1)S(1)} collective-permute-done((bf16[8,384]{1,0:T(8,128)(2,1)S(1)}, bf16[8,384]{1,0:T(8,128)(2,1)S(1)}, u32[]{:S(2)}, u32[]{:S(2)}) %collective-permute-start.9) | collective-permute-done | bytes 6176 | tf_op jit(solution)/shard_map/ppermute | solution.py:34
  137.6 1.9 %collective-permute-start.10 = (bf16[4,64,768]{2,1,0:T(8,128)(2,1)S(1)}, bf16[4,64,768]{2,1,0:T(8,128)(2,1)S(1)}, u32[]{:S(2)}, u32[]{:S(2)}) collective-permute-start(bf16[4,64,768]{2,1,0:T(8,128)(2,1)S(1)} %get-tuple-element.62), channel_id=1, source_target_pairs={{0,1},{1,0},{2,3},{3,2},{4,5},{5,4},{6,7},{7,6},{8,9},{9,8},{10,11... | collective-permute-start | bytes 1179656 | tf_op jit(solution)/shard_map/ppermute | solution.py:43
  139.5 1.3 collective-permute-done.10.right_ref
  141.8 7.0 %all-to-all-start.5 = ((bf16[8,24,640]{2,1,0:T(8,128)(2,1)}), bf16[8,24,640]{2,1,0:T(8,128)(2,1)S(1)}, u32[]{:S(2)}, u32[]{:S(2)}) async-start(bf16[8,24,640]{2,1,0:T(8,128)(2,1)} %reduce_sum.12), calls=%async_computation.5 | async-start | bytes 491520 | tf_op jit(solution)/shard_map/all_to_all | solution.py:507
  148.8 3.1 %collective-permute-start.13 = (bf16[64,768]{1,0:T(8,128)(2,1)S(1)}, bf16[64,768]{1,0:T(8,128)(2,1)S(1)}, u32[]{:S(2)}, u32[]{:S(2)}) collective-permute-start(bf16[64,768]{1,0:T(8,128)(2,1)S(1)} %get-tuple-element.77), channel_id=1, source_target_pairs={{0,6},{2,0},{4,2},{6,4},{1,7},{3,1},{5,3},{7,5},{8,14},{10,8},{12,... | collective-permute-start | bytes 294920 | tf_op jit(solution)/shard_map/ppermute | solution.py:39
  152.6 1.8 collective-permute-done.13
  154.4 2.8 %collective-permute-done.12 = bf16[64,768]{1,0:T(8,128)(2,1)S(1)} collective-permute-done((bf16[64,768]{1,0:T(8,128)(2,1)S(1)}, bf16[64,768]{1,0:T(8,128)(2,1)S(1)}, u32[]{:S(2)}, u32[]{:S(2)}) %collective-permute-start.12) | collective-permute-done | bytes 98336 | tf_op jit(solution)/shard_map/ppermute | solution.py:39
  157.2 2.4 %collective-permute-done.11 = bf16[64,768]{1,0:T(8,128)(2,1)S(1)} collective-permute-done((bf16[64,768]{1,0:T(8,128)(2,1)S(1)}, bf16[64,768]{1,0:T(8,128)(2,1)S(1)}, u32[]{:S(2)}, u32[]{:S(2)}) %collective-permute-start.11) | collective-permute-done | bytes 98336 | tf_op jit(solution)/shard_map/ppermute | solution.py:39
  159.7 12.3 %all_to_all.36.shares_ref = bf16[8,24,640]{2,1,0:T(8,128)(2,1)S(1)} all-to-all(bf16[8,24,640]{2,1,0:T(8,128)(2,1)S(1)} %shard_map.179), channel_id=1, replica_groups=mesh['z'=8,'y'=4,'x'=4,'c'=2] {'x','c'}, dimensions={0} | all-to-all | bytes 491520 | tf_op jit(solution)/shard_map/all_to_all | solution.py:510
  (65 shorter events, 19.2 us)
Async XLA Ops:
  7.2 33.7 %all-gather.5.cloned.1.call-start = ((), (), s32[]{:S(2)}) async-start(), calls=%async_computation.7 | async-start | bytes 1327104 | tf_op jit(solution)/shard_map/all_gather | solution.py:432
  29.2 15.6 %all-to-all-start.1 = ((bf16[4,8,24,640]{3,2,1,0:T(8,128)(2,1)}), bf16[4,8,24,640]{3,2,1,0:T(8,128)(2,1)S(1)}, u32[]{:S(2)}, u32[]{:S(2)}) async-start(bf16[4,8,24,640]{3,2,1,0:T(8,128)(2,1)} %broadcast_in_dim.11), calls=%async_computation.1 | async-start | bytes 1966080 | tf_op jit(solution)/shard_map/all_to_all | solution.py:429
  33.3 47.0 %all-gather.7.cloned.1.call-start = ((), (), s32[]{:S(2)}) async-start(), calls=%async_computation.8 | async-start | bytes 3538944 | tf_op jit(solution)/shard_map/all_gather | solution.py:442
  40.8 6.0 %copy-start.2 = (bf16[768,768]{1,0:T(8,128)(2,1)S(1)}, bf16[768,768]{1,0:T(8,128)(2,1)}, u32[]{:S(2)}) copy-start(bf16[768,768]{1,0:T(8,128)(2,1)} %all-gather.5.cloned.1.call-done) | copy-start | bytes 3538948
  41.9 4.9 %collective-permute-start = (bf16[8,768]{1,0:T(8,128)(2,1)S(1)}, bf16[8,768]{1,0:T(8,128)(2,1)S(1)}, u32[]{:S(2)}, u32[]{:S(2)}) collective-permute-start(bf16[8,768]{1,0:T(8,128)(2,1)S(1)} %fusion.15), channel_id=1, source_target_pairs={{6,14},{7,15},{8,0},{9,1},{14,22},{15,23},{16,8},{17,9},{22,30},{2... | collective-permute-start | bytes 36872 | tf_op jit(solution)/shard_map/ppermute | solution.py:34
  45.5 10.0 %copy-start.10 = (s32[1,128]{1,0:T(1,128)S(1)}, s32[1,128]{1,0:T(1,128)}, u32[]{:S(2)}) copy-start(s32[1,128]{1,0:T(1,128)} %param.13) | copy-start | bytes 1540
  47.8 0.8 copy-start.5
  48.5 7.1 %copy-start.9 = (s32[1,128]{1,0:T(1,128)S(1)}, s32[1,128]{1,0:T(1,128)}, u32[]{:S(2)}) copy-start(s32[1,128]{1,0:T(1,128)} %param.14) | copy-start | bytes 1540
  48.5 7.3 %copy-start.8 = (bf16[1,128,367]{1,2,0:T(8,128)(2,1)S(1)}, bf16[1,128,367]{1,2,0:T(8,128)(2,1)}, u32[]{:S(2)}) copy-start(bf16[1,128,367]{1,2,0:T(8,128)(2,1)} %param.21) | copy-start | bytes 281860
  48.5 15.1 %copy-start.7 = (bf16[1,128,768]{2,1,0:T(8,128)(2,1)S(1)}, bf16[1,128,768]{2,1,0:T(8,128)(2,1)}, u32[]{:S(2)}) copy-start(bf16[1,128,768]{2,1,0:T(8,128)(2,1)} %param.12) | copy-start | bytes 589828
  48.5 15.1 %all-to-all-start.2 = ((bf16[8,64,384]{2,1,0:T(8,128)(2,1)}), bf16[8,64,384]{2,1,0:T(8,128)(2,1)S(1)}, u32[]{:S(2)}, u32[]{:S(2)}) async-start(bf16[8,64,384]{2,1,0:T(8,128)(2,1)} %copy-done.5), calls=%async_computation.2 | async-start | bytes 786432 | tf_op jit(solution)/shard_map/all_to_all | solution.py:443
  63.9 5.5 %collective-permute-start.1 = (bf16[128,768]{1,0:T(8,128)(2,1)S(1)}, bf16[128,768]{1,0:T(8,128)(2,1)S(1)}, u32[]{:S(2)}, u32[]{:S(2)}) collective-permute-start(bf16[128,768]{1,0:T(8,128)(2,1)S(1)} %get-tuple-element.46), channel_id=1, source_target_pairs={{0,8},{8,16},{16,24},{24,32},{32,40},{40,48},{48,56},{56,64},{64,7... | collective-permute-start | bytes 589832 | tf_op jit(solution)/shard_map/ppermute | solution.py:22
  66.1 7.2 %collective-permute-start.2 = (bf16[128,768]{1,0:T(8,128)(2,1)S(1)}, bf16[128,768]{1,0:T(8,128)(2,1)S(1)}, u32[]{:S(2)}, u32[]{:S(2)}) collective-permute-start(bf16[128,768]{1,0:T(8,128)(2,1)S(1)} %get-tuple-element.46), channel_id=1, source_target_pairs={{8,0},{16,8},{24,16},{32,24},{40,32},{48,40},{56,48},{64,56},{72,6... | collective-permute-start | bytes 589832 | tf_op jit(solution)/shard_map/ppermute | solution.py:22
  80.3 1.9 %copy-start = (bf16[6144,256]{1,0:T(8,128)(2,1)S(1)}, bf16[6144,256]{1,0:T(8,128)(2,1)}, u32[]{:S(2)}) copy-start(bf16[6144,256]{1,0:T(8,128)(2,1)} %all-gather.7.cloned.1.call-done) | copy-start | bytes 9437188
  82.2 8.2 %copy-start.1 = (bf16[6144,256]{1,0:T(8,128)(2,1)S(1)}, bf16[6144,256]{1,0:T(8,128)(2,1)}, u32[]{:S(2)}) copy-start(bf16[6144,256]{1,0:T(8,128)(2,1)} %all-gather.7.cloned.1.call-done) | copy-start | bytes 9437188
  83.6 6.9 %copy-start.6 = (bf16[1,128,768]{2,1,0:T(8,128)(2,1)S(1)}, bf16[1,128,768]{2,1,0:T(8,128)(2,1)}, u32[]{:S(2)}) copy-start(bf16[1,128,768]{2,1,0:T(8,128)(2,1)} %param.20) | copy-start | bytes 589828
  83.7 13.4 %collective-permute-start.7 = (bf16[128,768]{1,0:T(8,128)(2,1)S(1)}, bf16[128,768]{1,0:T(8,128)(2,1)S(1)}, u32[]{:S(2)}, u32[]{:S(2)}) collective-permute-start(bf16[128,768]{1,0:T(8,128)(2,1)S(1)} %get-tuple-element.81), channel_id=1, source_target_pairs={{0,6},{2,0},{4,2},{6,4},{1,7},{3,1},{5,3},{7,5},{8,14},{10,8},{12,... | collective-permute-start | bytes 589832 | tf_op jit(solution)/shard_map/ppermute | solution.py:39
  85.0 12.1 %collective-permute-start.6 = (bf16[128,768]{1,0:T(8,128)(2,1)S(1)}, bf16[128,768]{1,0:T(8,128)(2,1)S(1)}, u32[]{:S(2)}, u32[]{:S(2)}) collective-permute-start(bf16[128,768]{1,0:T(8,128)(2,1)S(1)} %get-tuple-element.82), channel_id=1, source_target_pairs={{0,4},{2,6},{4,0},{6,2},{1,5},{3,7},{5,1},{7,3},{8,12},{10,14},{12... | collective-permute-start | bytes 589832 | tf_op jit(solution)/shard_map/ppermute | solution.py:39
  85.7 11.9 %collective-permute-start.5 = (bf16[128,768]{1,0:T(8,128)(2,1)S(1)}, bf16[128,768]{1,0:T(8,128)(2,1)S(1)}, u32[]{:S(2)}, u32[]{:S(2)}) collective-permute-start(bf16[128,768]{1,0:T(8,128)(2,1)S(1)} %get-tuple-element.83), channel_id=1, source_target_pairs={{0,2},{2,4},{4,6},{6,0},{1,3},{3,5},{5,7},{7,1},{8,10},{10,12},{12... | collective-permute-start | bytes 589832 | tf_op jit(solution)/shard_map/ppermute | solution.py:39
  86.1 5.7 %collective-permute-start.3 = (bf16[80,768]{1,0:T(8,128)(2,1)S(1)}, bf16[80,768]{1,0:T(8,128)(2,1)S(1)}, u32[]{:S(2)}, u32[]{:S(2)}) collective-permute-start(bf16[80,768]{1,0:T(8,128)(2,1)S(1)} %get-tuple-element.53), channel_id=1, source_target_pairs={{0,8},{8,16},{16,24},{24,32},{32,40},{40,48},{48,56},{56,64},{64,7... | collective-permute-start | bytes 368648 | tf_op jit(solution)/shard_map/ppermute | solution.py:22
  89.2 5.9 %collective-permute-start.4 = (bf16[80,768]{1,0:T(8,128)(2,1)S(1)}, bf16[80,768]{1,0:T(8,128)(2,1)S(1)}, u32[]{:S(2)}, u32[]{:S(2)}) collective-permute-start(bf16[80,768]{1,0:T(8,128)(2,1)S(1)} %get-tuple-element.54), channel_id=1, source_target_pairs={{8,0},{16,8},{24,16},{32,24},{40,32},{48,40},{56,48},{64,56},{72,6... | collective-permute-start | bytes 368648 | tf_op jit(solution)/shard_map/ppermute | solution.py:22
  97.7 19.8 %all-to-all-start.3 = ((bf16[8,64,896]{2,1,0:T(8,128)(2,1)}), bf16[8,64,896]{2,1,0:T(8,128)(2,1)S(1)}, u32[]{:S(2)}, u32[]{:S(2)}) async-start(bf16[8,64,896]{2,1,0:T(8,128)(2,1)} %get-tuple-element.59), calls=%async_computation.3 | async-start | bytes 1835008 | tf_op jit(solution)/shard_map/all_to_all | solution.py:483
  103.8 2.3 %collective-permute-start.8 = (bf16[4,128,768]{2,1,0:T(8,128)(2,1)S(1)}, bf16[4,128,768]{2,1,0:T(8,128)(2,1)S(1)}, u32[]{:S(2)}, u32[]{:S(2)}) collective-permute-start(bf16[4,128,768]{2,1,0:T(8,128)(2,1)S(1)} %pad_maximum_fusion.near_ref), channel_id=1, source_target_pairs={{0,1},{1,0},{2,3},{3,2},{4,5},{5,4},{6,7},{7,6},{8,9},{9,8},{10,11... | collective-permute-start | bytes 2359304 | tf_op jit(solution)/shard_map/ppermute | solution.py:43
  106.0 0.9 copy-start.3
  117.4 1.1 copy-start.4
  120.8 20.1 %all-to-all-start.4 = ((bf16[4,8,24,640]{3,2,1,0:T(8,128)(2,1)}), bf16[4,8,24,640]{3,2,1,0:T(8,128)(2,1)S(1)}, u32[]{:S(2)}, u32[]{:S(2)}) async-start(bf16[4,8,24,640]{3,2,1,0:T(8,128)(2,1)} %shard_map.176), calls=%async_computation.4 | async-start | bytes 1966080 | tf_op jit(solution)/shard_map/all_to_all | solution.py:505
  126.7 10.0 %collective-permute-start.9 = (bf16[8,384]{1,0:T(8,128)(2,1)S(1)}, bf16[8,384]{1,0:T(8,128)(2,1)S(1)}, u32[]{:S(2)}, u32[]{:S(2)}) collective-permute-start(bf16[8,384]{1,0:T(8,128)(2,1)S(1)} %fusion.16), channel_id=1, source_target_pairs={{0,8},{1,9},{8,16},{9,17},{14,6},{15,7},{16,24},{17,25},{22,14},{2... | collective-permute-start | bytes 18440 | tf_op jit(solution)/shard_map/ppermute | solution.py:34
  137.6 3.3 %collective-permute-start.10 = (bf16[4,64,768]{2,1,0:T(8,128)(2,1)S(1)}, bf16[4,64,768]{2,1,0:T(8,128)(2,1)S(1)}, u32[]{:S(2)}, u32[]{:S(2)}) collective-permute-start(bf16[4,64,768]{2,1,0:T(8,128)(2,1)S(1)} %get-tuple-element.62), channel_id=1, source_target_pairs={{0,1},{1,0},{2,3},{3,2},{4,5},{5,4},{6,7},{7,6},{8,9},{9,8},{10,11... | collective-permute-start | bytes 1179656 | tf_op jit(solution)/shard_map/ppermute | solution.py:43
  141.8 17.8 %all-to-all-start.5 = ((bf16[8,24,640]{2,1,0:T(8,128)(2,1)}), bf16[8,24,640]{2,1,0:T(8,128)(2,1)S(1)}, u32[]{:S(2)}, u32[]{:S(2)}) async-start(bf16[8,24,640]{2,1,0:T(8,128)(2,1)} %reduce_sum.12), calls=%async_computation.5 | async-start | bytes 491520 | tf_op jit(solution)/shard_map/all_to_all | solution.py:507
  148.8 5.6 %collective-permute-start.13 = (bf16[64,768]{1,0:T(8,128)(2,1)S(1)}, bf16[64,768]{1,0:T(8,128)(2,1)S(1)}, u32[]{:S(2)}, u32[]{:S(2)}) collective-permute-start(bf16[64,768]{1,0:T(8,128)(2,1)S(1)} %get-tuple-element.77), channel_id=1, source_target_pairs={{0,6},{2,0},{4,2},{6,4},{1,7},{3,1},{5,3},{7,5},{8,14},{10,8},{12,... | collective-permute-start | bytes 294920 | tf_op jit(solution)/shard_map/ppermute | solution.py:39
  151.9 5.3 %collective-permute-start.12 = (bf16[64,768]{1,0:T(8,128)(2,1)S(1)}, bf16[64,768]{1,0:T(8,128)(2,1)S(1)}, u32[]{:S(2)}, u32[]{:S(2)}) collective-permute-start(bf16[64,768]{1,0:T(8,128)(2,1)S(1)} %get-tuple-element.78), channel_id=1, source_target_pairs={{0,4},{2,6},{4,0},{6,2},{1,5},{3,7},{5,1},{7,3},{8,12},{10,14},{12... | collective-permute-start | bytes 294920 | tf_op jit(solution)/shard_map/ppermute | solution.py:39
  151.9 7.7 %collective-permute-start.11 = (bf16[64,768]{1,0:T(8,128)(2,1)S(1)}, bf16[64,768]{1,0:T(8,128)(2,1)S(1)}, u32[]{:S(2)}, u32[]{:S(2)}) collective-permute-start(bf16[64,768]{1,0:T(8,128)(2,1)S(1)} %get-tuple-element.79), channel_id=1, source_target_pairs={{0,2},{2,4},{4,6},{6,0},{1,3},{3,5},{5,7},{7,1},{8,10},{10,12},{12... | collective-permute-start | bytes 294920 | tf_op jit(solution)/shard_map/ppermute | solution.py:39
Sparse Core Ops, SparseCore 0:
  10.4 30.3 all-gather.4
  48.7 31.6 all-gather.6

commit v3 on v2

--- a/solution.py
+++ b/solution.py
@@ -224,22 +224,9 @@
     return one_hot(lax.broadcasted_iota(jnp.int32, (16, CHUNK), 1) == column)
 
 
-def base_body(product_ref, chunks_ref, place_ref, fine_ref, scores_ref, base_ref):
-    rows = fine_ref.shape[0]
-    product = product_ref[...]
-    tracks = scores_ref.shape[0]
-    scores_ref[:CHUNK] = mm(product, chunks_ref[6]).T.astype(BF)
-    scores_ref[CHUNK:] = mm(product, chunks_ref[7]).T[: tracks - CHUNK].astype(BF)
-    place = place_ref[...]
-    total = mm(split_hot(rows, True), fine_ref[...])
-    for index in range(3):
-        total = total + mm_nt(place[:, index * CHUNK : (index + 1) * CHUNK], chunks_ref[index])
-    base_ref[...] = total
-
-
 def skip_body(
-    base_ref, own_ref, chunks_ref, low_ref, high_ref, pre_ref, gain_ref, place_ref, score_ref,
-    skip_ref, out_ref,
+    product_ref, fine_ref, own_ref, chunks_ref, low_ref, high_ref, pre_ref, gain_ref, place_ref, score_ref,
+    skip_ref, out_ref, scores_ref,
 ):
     rows = pre_ref.shape[0]
     half_rows = rows // 2
@@ -251,8 +238,14 @@
         asked = ref[half_rows:, :rows].astype(F32)[:1, :half_rows].astype(jnp.int32)
         acceptor = acceptor + mm(one_hot(numbers == asked), ref[:half_rows])
     acceptor = acceptor.astype(BF)
-    grad = base_ref[...]
+    product = product_ref[...]
+    tracks = scores_ref.shape[0]
+    scores_ref[:CHUNK] = mm(product, chunks_ref[6]).T.astype(BF)
+    scores_ref[CHUNK:] = mm(product, chunks_ref[7]).T[: tracks - CHUNK].astype(BF)
+    place = place_ref[...]
+    grad = mm(split_hot(rows, True), fine_ref[...])
     for index in range(3):
+        grad = grad + mm_nt(place[:, index * CHUNK : (index + 1) * CHUNK], chunks_ref[index])
         grad = grad + mm_nt(
             acceptor[:, index * CHUNK : (index + 1) * CHUNK], chunks_ref[3 + index]
         )
@@ -470,15 +463,11 @@
     left_near = jnp.stack(
         left_near[:1] + [send_x(left_near[step], step) for step in range(1, nx)], 0
     )
-    scores, base = call(
-        base_body, [((tracks, pairs), BF), (fine_shape, F32)], product, chunks, place_donor, fine_grad[0]
-    )
-    skip_out, outgoing = call(
+    skip_out, outgoing, scores = call(
         skip_body,
-        [(fine_shape, BF), ((group_size, half_rows, half + 2 * CHUNK), BF)],
-        base, own_grads, chunks, grads_low, grads_high, pre_norm, gain_rows, place_donor, score_grad[0],
-    )
-    outgoing, left_near = lax.optimization_barrier((outgoing, left_near))
+        [(fine_shape, BF), ((group_size, half_rows, half + 2 * CHUNK), BF), ((tracks, pairs), BF)],
+        product, fine_grad[0], own_grads, chunks, grads_low, grads_high, pre_norm, gain_rows, place_donor, score_grad[0],
+    )
     left_far = swap_core(left_near)
     grads = lax.all_to_all(outgoing, GROUP, 0, 0, tiled=True)
     tap_grads = grads[:, :, :half]

time: 181 us -> 181 us (level)
  local copies, waits for them, and re-layouts: 8 us -> 5.98 us
    ppermute x6, waiting for transfers between devices: 7.49 us -> 4.66 us  [send_x(): lax.ppermute(block, 'x', [(i, (i + step) % count) for i in range(count)])]
    ppermute x2, waiting for transfers between devices: 3.63 us -> 1.35 us  [swap_core(): return lax.ppermute(block, 'c', [(0, 1), (1, 0)])]
    unnamed x23 -> x17, local copies, waits for them, and re-layouts: 4.79 us -> 2.77 us
    all_to_all x1, waiting for transfers between devices: 10.5 us -> 12.4 us  [local(): grads = lax.all_to_all(outgoing, GROUP, 0, 0, tiled=True)]
    pallas_call x11 -> x10, Pallas kernels: 11.8 us -> 12 us  [call(): pl.pallas_call(body, out_shape=[jax.ShapeDtypeStruct(shape, kind) for sha...]
  transfers between devices with their start and end apart: 21 -> 21, of which waited for: 16 -> 16; matrix products, arithmetic and copies ran while one was open for 2% -> 3% of each run, Pallas kernels for 3% -> 2%
where the time goes in v3:
time: 181 us; the launch traced here: 180 us
  waiting for transfers between devices  61.1 us (34%)
  starting transfers between devices  52.1 us (29%)
  blocking collectives  32.5 us (18%)
  between operations  14.3 us (8%)
  Pallas kernels  12 us (7%)
  local copies, waits for them, and re-layouts  5.98 us (3%)
  other arithmetic  2.31 us (1%)
    all_to_all x1, blocking collectives, local(): both = lax.all_to_all(both, 'z', 0, 0, tiled=True)  19 us
    all_to_all x1, blocking collectives, local(): shares = lax.all_to_all(shares, GROUP, 0, 0, tiled=True)  13.5 us
    all_to_all x1, waiting for transfers between devices, local(): grads = lax.all_to_all(outgoing, GROUP, 0, 0, tiled=True)  12.4 us
    pallas_call x10, Pallas kernels, call(): pl.pallas_call(body, out_shape=[jax.ShapeDtypeStruct(shape, kind) for sha...  12 us
    ppermute x4, waiting for transfers between devices, send_seq(): return lax.ppermute(block, SEQ, pairs)  10.6 us
    ppermute x2, waiting for transfers between devices, send_edge(): return lax.ppermute(block, AXES, pairs)  7.94 us
    ppermute x6, starting transfers between devices, send_x(): lax.ppermute(block, 'x', [(i, (i + step) % count) for i in range(count)])  7.86 us
    ppermute x4, starting transfers between devices, send_seq(): return lax.ppermute(block, SEQ, pairs)  7.85 us
  transfers between devices with their start and end apart: 21, of which 16 were waited for; matrix products, arithmetic and copies ran while one was open for 3% of the time, Pallas kernels for 2%

profile of v3, /device:TPU:1, one launch (start us, length us, event | category | flops | bytes accessed | tf_op | source)
XLA Modules:
  0.0 180.4 jit_solution(8866534994523983625)
XLA Ops:
  7.2 1.9 %shard_map.170 = (bf16[8,24,640]{2,1,0:T(8,128)(2,1)}, bf16[96,768]{1,0:T(8,128)(2,1)}) custom-call(bf16[24,4,768]{2,1,0:T(4,128)(2,1)} %conv_ref.1, bf16[24,768]{1,0:T(8,128)(2,1)} %donor_ref.1, bf16[24,768]{1,0:T(8,128)(2,1)} %acceptor_ref.1, bf16[24,367]{1,0:T(8,128)(2,1)} %track_ref.1, bf16[1,24]{1,0:T(2,128)(2,1)} %bitcast.51, bf16[64,768]{1,0:T(8,128)(2,1)} %bitcast.50), custom_call_target="tpu_custom_call" | custom-call | tf_op jit(solution)/shard_map/pallas_call | solution.py:60
  9.1 19.0 %all_to_all.35 = bf16[8,24,640]{2,1,0:T(8,128)(2,1)S(1)} all-to-all(bf16[8,24,640]{2,1,0:T(8,128)(2,1)} %get-tuple-element.37), channel_id=1, replica_groups=mesh['z'=8,'y'=4,'x'=4,'c'=2] {'z'}, dimensions={0} | all-to-all | bytes 491520 | tf_op jit(solution)/shard_map/all_to_all | solution.py:419
  29.2 4.2 %all-to-all-start.1 = ((bf16[4,8,24,640]{3,2,1,0:T(8,128)(2,1)}), bf16[4,8,24,640]{3,2,1,0:T(8,128)(2,1)S(1)}, u32[]{:S(2)}, u32[]{:S(2)}) async-start(bf16[4,8,24,640]{3,2,1,0:T(8,128)(2,1)} %broadcast_in_dim.11), calls=%async_computation.1 | async-start | bytes 1966080 | tf_op jit(solution)/shard_map/all_to_all | solution.py:422
  33.4 7.5 %all-gather.5.cloned.1.call-done = bf16[768,768]{1,0:T(8,128)(2,1)} async-done(((bf16[96,768]{1,0:T(8,128)(2,1)}), bf16[768,768]{1,0:T(8,128)(2,1)}) %all-gather.5.cloned.1.call-update) | async-done | bytes 1179664 | tf_op jit(solution)/shard_map/all_gather | solution.py:425
  41.9 1.3 collective-permute-start
  43.2 1.5 all-to-all-done.1.both_ref
  45.5 1.3 collective-permute-done.edge_ref
  48.5 7.0 %all-to-all-start.2 = ((bf16[8,64,384]{2,1,0:T(8,128)(2,1)}), bf16[8,64,384]{2,1,0:T(8,128)(2,1)S(1)}, u32[]{:S(2)}, u32[]{:S(2)}) async-start(bf16[8,64,384]{2,1,0:T(8,128)(2,1)} %copy-done.2), calls=%async_computation.2 | async-start | bytes 786432 | tf_op jit(solution)/shard_map/all_to_all | solution.py:436
  56.1 7.5 %all-to-all-done.2.taps_ref = bf16[8,64,384]{2,1,0:T(8,128)(2,1)S(1)} async-done(((bf16[8,64,384]{2,1,0:T(8,128)(2,1)}), bf16[8,64,384]{2,1,0:T(8,128)(2,1)S(1)}, u32[]{:S(2)}, u32[]{:S(2)}) %all-to-all-start.2) | async-done | bytes 393248 | tf_op jit(solution)/shard_map/all_to_all | solution.py:436
  63.9 2.2 %collective-permute-start.1 = (bf16[128,768]{1,0:T(8,128)(2,1)S(1)}, bf16[128,768]{1,0:T(8,128)(2,1)S(1)}, u32[]{:S(2)}, u32[]{:S(2)}) collective-permute-start(bf16[128,768]{1,0:T(8,128)(2,1)S(1)} %get-tuple-element.43), channel_id=1, source_target_pairs={{0,8},{8,16},{16,24},{24,32},{32,40},{40,48},{48,56},{56,64},{64,7... | collective-permute-start | bytes 589832 | tf_op jit(solution)/shard_map/ppermute | solution.py:22
  66.1 1.3 collective-permute-start.2
  67.4 2.0 %collective-permute-done.1.low_ref = bf16[128,768]{1,0:T(8,128)(2,1)S(1)} collective-permute-done((bf16[128,768]{1,0:T(8,128)(2,1)S(1)}, bf16[128,768]{1,0:T(8,128)(2,1)S(1)}, u32[]{:S(2)}, u32[]{:S(2)}) %collective-permute-start.1) | collective-permute-done | bytes 196640 | tf_op jit(solution)/shard_map/ppermute | solution.py:22
  69.4 3.9 %collective-permute-done.2.high_ref = bf16[128,768]{1,0:T(8,128)(2,1)S(1)} collective-permute-done((bf16[128,768]{1,0:T(8,128)(2,1)S(1)}, bf16[128,768]{1,0:T(8,128)(2,1)S(1)}, u32[]{:S(2)}, u32[]{:S(2)}) %collective-permute-start.2) | collective-permute-done | bytes 196640 | tf_op jit(solution)/shard_map/ppermute | solution.py:22
  73.3 7.0 %all-gather.7.cloned.1.call-done = bf16[6144,256]{1,0:T(8,128)(2,1)} async-done(((bf16[768,256]{1,0:T(8,128)(2,1)}), bf16[6144,256]{1,0:T(8,128)(2,1)}) %all-gather.7.cloned.1.call-update) | async-done | bytes 3145744 | tf_op jit(solution)/shard_map/all_gather | solution.py:435
  80.3 1.9 %copy-done = bf16[6144,256]{1,0:T(8,128)(2,1)S(1)} copy-done((bf16[6144,256]{1,0:T(8,128)(2,1)S(1)}, bf16[6144,256]{1,0:T(8,128)(2,1)}, u32[]{:S(2)}) %copy-start) | copy-done | bytes 3145752
  82.2 1.3 shard_map.173
  83.9 2.3 %collective-permute-start.6 = (bf16[128,768]{1,0:T(8,128)(2,1)S(1)}, bf16[128,768]{1,0:T(8,128)(2,1)}, u32[]{:S(2)}, u32[]{:S(2)}) collective-permute-start(bf16[128,768]{1,0:T(8,128)(2,1)S(1)} %get-tuple-element.76), channel_id=1, source_target_pairs={{0,4},{2,6},{4,0},{6,2},{1,5},{3,7},{5,1},{7,3},{8,12},{10,14},{12... | collective-permute-start | bytes 589832 | tf_op jit(solution)/shard_map/ppermute | solution.py:39
  87.3 3.1 %collective-permute-start.3 = (bf16[80,768]{1,0:T(8,128)(2,1)S(1)}, bf16[80,768]{1,0:T(8,128)(2,1)S(1)}, u32[]{:S(2)}, u32[]{:S(2)}) collective-permute-start(bf16[80,768]{1,0:T(8,128)(2,1)S(1)} %get-tuple-element.46), channel_id=1, source_target_pairs={{0,8},{8,16},{16,24},{24,32},{32,40},{40,48},{48,56},{56,64},{64,7... | collective-permute-start | bytes 368648 | tf_op jit(solution)/shard_map/ppermute | solution.py:22
  92.2 4.2 %collective-permute-done.4.high_ref = bf16[80,768]{1,0:T(8,128)(2,1)S(1)} collective-permute-done((bf16[80,768]{1,0:T(8,128)(2,1)S(1)}, bf16[80,768]{1,0:T(8,128)(2,1)S(1)}, u32[]{:S(2)}, u32[]{:S(2)}) %collective-permute-start.4) | collective-permute-done | bytes 122912 | tf_op jit(solution)/shard_map/ppermute | solution.py:22
  96.4 2.4 %shard_map.174 = (bf16[128,768]{1,0:T(8,128)(2,1)}, bf16[8,64,896]{2,1,0:T(8,128)(2,1)}, bf16[367,128]{1,0:T(8,128)(2,1)}) custom-call(bf16[128,768]{1,0:T(8,128)(2,1)S(1)} %get-tuple-element.44.product_ref, bf16[128,768]{1,0:T(8,128)(2,1)S(1)} %bitcast.43, f32[128,768]{1,0:T(8,128)S(1)} %get-tuple-element.45.own_ref, bf16[8,768,256]{2,1,0:T(8,128)(2,1)S(1)} %bitcast.38, ...), custom_call_target="tpu_custom_call" | custom-call | tf_op jit(solution)/shard_map/pallas_call | solution.py:60
  98.8 5.6 %all-to-all-start.3 = ((bf16[8,64,896]{2,1,0:T(8,128)(2,1)}), bf16[8,64,896]{2,1,0:T(8,128)(2,1)S(1)}, u32[]{:S(2)}, u32[]{:S(2)}) async-start(bf16[8,64,896]{2,1,0:T(8,128)(2,1)} %get-tuple-element.53), calls=%async_computation.3 | async-start | bytes 1835008 | tf_op jit(solution)/shard_map/all_to_all | solution.py:472
  105.7 12.4 %all-to-all-done.3.grads_ref = bf16[8,64,896]{2,1,0:T(8,128)(2,1)S(1)} async-done(((bf16[8,64,896]{2,1,0:T(8,128)(2,1)}), bf16[8,64,896]{2,1,0:T(8,128)(2,1)S(1)}, u32[]{:S(2)}, u32[]{:S(2)}) %all-to-all-start.3) | async-done | bytes 917536 | tf_op jit(solution)/shard_map/all_to_all | solution.py:472
  118.1 3.3 %shard_map.175 = bf16[4,8,24,640]{3,2,1,0:T(8,128)(2,1)} custom-call(bf16[512,768]{1,0:T(8,128)(2,1)S(1)} %get-tuple-element.51.left_ref, bf16[4,128,768]{2,1,0:T(8,128)(2,1)S(1)} %pad_maximum_fusion.near_ref, bf16[4,128,768]{2,1,0:T(8,128)(2,1)} %collective-permute-done.8.far_ref, bf16[8,64,896]{2,1,0:T(8,128)(2,1)S(1)} %all-to-all-done.3.grads_ref), custom_call_target="tpu_custom_call" | custom-call | tf_op jit(solution)/shard_map/pallas_call | solution.py:60
  121.4 5.8 %all-to-all-start.4 = ((bf16[4,8,24,640]{3,2,1,0:T(8,128)(2,1)}), bf16[4,8,24,640]{3,2,1,0:T(8,128)(2,1)S(1)}, u32[]{:S(2)}, u32[]{:S(2)}) async-start(bf16[4,8,24,640]{3,2,1,0:T(8,128)(2,1)} %shard_map.175), calls=%async_computation.4 | async-start | bytes 1966080 | tf_op jit(solution)/shard_map/all_to_all | solution.py:494
  127.3 3.4 %collective-permute-start.9 = (bf16[8,384]{1,0:T(8,128)(2,1)S(1)}, bf16[8,384]{1,0:T(8,128)(2,1)S(1)}, u32[]{:S(2)}, u32[]{:S(2)}) collective-permute-start(bf16[8,384]{1,0:T(8,128)(2,1)S(1)} %fusion.16), channel_id=1, source_target_pairs={{0,8},{1,9},{8,16},{9,17},{14,6},{15,7},{16,24},{17,25},{22,14},{2... | collective-permute-start | bytes 18440 | tf_op jit(solution)/shard_map/ppermute | solution.py:34
  130.7 6.6 %collective-permute-done.9.edge_ref = bf16[8,384]{1,0:T(8,128)(2,1)S(1)} collective-permute-done((bf16[8,384]{1,0:T(8,128)(2,1)S(1)}, bf16[8,384]{1,0:T(8,128)(2,1)S(1)}, u32[]{:S(2)}, u32[]{:S(2)}) %collective-permute-start.9) | collective-permute-done | bytes 6176 | tf_op jit(solution)/shard_map/ppermute | solution.py:34
  138.2 1.9 %collective-permute-start.10 = (bf16[4,64,768]{2,1,0:T(8,128)(2,1)S(1)}, bf16[4,64,768]{2,1,0:T(8,128)(2,1)S(1)}, u32[]{:S(2)}, u32[]{:S(2)}) collective-permute-start(bf16[4,64,768]{2,1,0:T(8,128)(2,1)S(1)} %get-tuple-element.56), channel_id=1, source_target_pairs={{0,1},{1,0},{2,3},{3,2},{4,5},{5,4},{6,7},{7,6},{8,9},{9,8},{10,11... | collective-permute-start | bytes 1179656 | tf_op jit(solution)/shard_map/ppermute | solution.py:43
  140.1 1.3 collective-permute-done.10.right_ref
  142.4 7.0 %all-to-all-start.5 = ((bf16[8,24,640]{2,1,0:T(8,128)(2,1)}), bf16[8,24,640]{2,1,0:T(8,128)(2,1)S(1)}, u32[]{:S(2)}, u32[]{:S(2)}) async-start(bf16[8,24,640]{2,1,0:T(8,128)(2,1)} %reduce_sum.12), calls=%async_computation.5 | async-start | bytes 491520 | tf_op jit(solution)/shard_map/all_to_all | solution.py:496
  149.5 4.2 %collective-permute-start.12 = (bf16[64,768]{1,0:T(8,128)(2,1)S(1)}, bf16[64,768]{1,0:T(8,128)(2,1)S(1)}, u32[]{:S(2)}, u32[]{:S(2)}) collective-permute-start(bf16[64,768]{1,0:T(8,128)(2,1)S(1)} %get-tuple-element.72), channel_id=1, source_target_pairs={{0,4},{2,6},{4,0},{6,2},{1,5},{3,7},{5,1},{7,3},{8,12},{10,14},{12... | collective-permute-start | bytes 294920 | tf_op jit(solution)/shard_map/ppermute | solution.py:39
  154.5 3.3 %collective-permute-done.12 = bf16[64,768]{1,0:T(8,128)(2,1)S(1)} collective-permute-done((bf16[64,768]{1,0:T(8,128)(2,1)S(1)}, bf16[64,768]{1,0:T(8,128)(2,1)S(1)}, u32[]{:S(2)}, u32[]{:S(2)}) %collective-permute-start.12) | collective-permute-done | bytes 98336 | tf_op jit(solution)/shard_map/ppermute | solution.py:39
  159.1 13.5 %all_to_all.36.shares_ref = bf16[8,24,640]{2,1,0:T(8,128)(2,1)S(1)} all-to-all(bf16[8,24,640]{2,1,0:T(8,128)(2,1)S(1)} %shard_map.178), channel_id=1, replica_groups=mesh['z'=8,'y'=4,'x'=4,'c'=2] {'x','c'}, dimensions={0} | all-to-all | bytes 491520 | tf_op jit(solution)/shard_map/all_to_all | solution.py:499
  (58 shorter events, 14.9 us)
Async XLA Ops:
  7.2 33.7 %all-gather.5.cloned.1.call-start = ((), (), s32[]{:S(2)}) async-start(), calls=%async_computation.7 | async-start | bytes 1327104 | tf_op jit(solution)/shard_map/all_gather | solution.py:425
  29.2 15.6 %all-to-all-start.1 = ((bf16[4,8,24,640]{3,2,1,0:T(8,128)(2,1)}), bf16[4,8,24,640]{3,2,1,0:T(8,128)(2,1)S(1)}, u32[]{:S(2)}, u32[]{:S(2)}) async-start(bf16[4,8,24,640]{3,2,1,0:T(8,128)(2,1)} %broadcast_in_dim.11), calls=%async_computation.1 | async-start | bytes 1966080 | tf_op jit(solution)/shard_map/all_to_all | solution.py:422
  33.4 47.0 %all-gather.7.cloned.1.call-start = ((), (), s32[]{:S(2)}) async-start(), calls=%async_computation.8 | async-start | bytes 3538944 | tf_op jit(solution)/shard_map/all_gather | solution.py:435
  40.8 6.0 %copy-start.1 = (bf16[768,768]{1,0:T(8,128)(2,1)S(1)}, bf16[768,768]{1,0:T(8,128)(2,1)}, u32[]{:S(2)}) copy-start(bf16[768,768]{1,0:T(8,128)(2,1)} %all-gather.5.cloned.1.call-done) | copy-start | bytes 3538948
  41.9 4.9 %collective-permute-start = (bf16[8,768]{1,0:T(8,128)(2,1)S(1)}, bf16[8,768]{1,0:T(8,128)(2,1)S(1)}, u32[]{:S(2)}, u32[]{:S(2)}) collective-permute-start(bf16[8,768]{1,0:T(8,128)(2,1)S(1)} %fusion.15), channel_id=1, source_target_pairs={{6,14},{7,15},{8,0},{9,1},{14,22},{15,23},{16,8},{17,9},{22,30},{2... | collective-permute-start | bytes 36872 | tf_op jit(solution)/shard_map/ppermute | solution.py:34
  45.5 10.0 %copy-start.7 = (s32[1,128]{1,0:T(1,128)S(1)}, s32[1,128]{1,0:T(1,128)}, u32[]{:S(2)}) copy-start(s32[1,128]{1,0:T(1,128)} %param.13) | copy-start | bytes 1540
  47.8 0.7 copy-start.2
  48.5 7.2 %copy-start.6 = (s32[1,128]{1,0:T(1,128)S(1)}, s32[1,128]{1,0:T(1,128)}, u32[]{:S(2)}) copy-start(s32[1,128]{1,0:T(1,128)} %param.14) | copy-start | bytes 1540
  48.5 7.3 %copy-start.5 = (bf16[1,128,367]{1,2,0:T(8,128)(2,1)S(1)}, bf16[1,128,367]{1,2,0:T(8,128)(2,1)}, u32[]{:S(2)}) copy-start(bf16[1,128,367]{1,2,0:T(8,128)(2,1)} %param.21) | copy-start | bytes 281860
  48.5 15.1 %copy-start.4 = (bf16[1,128,768]{2,1,0:T(8,128)(2,1)S(1)}, bf16[1,128,768]{2,1,0:T(8,128)(2,1)}, u32[]{:S(2)}) copy-start(bf16[1,128,768]{2,1,0:T(8,128)(2,1)} %param.12) | copy-start | bytes 589828
  48.5 15.1 %all-to-all-start.2 = ((bf16[8,64,384]{2,1,0:T(8,128)(2,1)}), bf16[8,64,384]{2,1,0:T(8,128)(2,1)S(1)}, u32[]{:S(2)}, u32[]{:S(2)}) async-start(bf16[8,64,384]{2,1,0:T(8,128)(2,1)} %copy-done.2), calls=%async_computation.2 | async-start | bytes 786432 | tf_op jit(solution)/shard_map/all_to_all | solution.py:436
  63.9 5.5 %collective-permute-start.1 = (bf16[128,768]{1,0:T(8,128)(2,1)S(1)}, bf16[128,768]{1,0:T(8,128)(2,1)S(1)}, u32[]{:S(2)}, u32[]{:S(2)}) collective-permute-start(bf16[128,768]{1,0:T(8,128)(2,1)S(1)} %get-tuple-element.43), channel_id=1, source_target_pairs={{0,8},{8,16},{16,24},{24,32},{32,40},{40,48},{48,56},{56,64},{64,7... | collective-permute-start | bytes 589832 | tf_op jit(solution)/shard_map/ppermute | solution.py:22
  66.1 7.2 %collective-permute-start.2 = (bf16[128,768]{1,0:T(8,128)(2,1)S(1)}, bf16[128,768]{1,0:T(8,128)(2,1)S(1)}, u32[]{:S(2)}, u32[]{:S(2)}) collective-permute-start(bf16[128,768]{1,0:T(8,128)(2,1)S(1)} %get-tuple-element.43), channel_id=1, source_target_pairs={{8,0},{16,8},{24,16},{32,24},{40,32},{48,40},{56,48},{64,56},{72,6... | collective-permute-start | bytes 589832 | tf_op jit(solution)/shard_map/ppermute | solution.py:22
  80.3 1.9 %copy-start = (bf16[6144,256]{1,0:T(8,128)(2,1)S(1)}, bf16[6144,256]{1,0:T(8,128)(2,1)}, u32[]{:S(2)}) copy-start(bf16[6144,256]{1,0:T(8,128)(2,1)} %all-gather.7.cloned.1.call-done) | copy-start | bytes 9437188
  83.6 12.8 %copy-start.3 = (bf16[1,128,768]{2,1,0:T(8,128)(2,1)S(1)}, bf16[1,128,768]{2,1,0:T(8,128)(2,1)}, u32[]{:S(2)}) copy-start(bf16[1,128,768]{2,1,0:T(8,128)(2,1)} %param.20) | copy-start | bytes 589828
  83.7 20.7 %collective-permute-start.5 = (bf16[128,768]{1,0:T(8,128)(2,1)S(1)}, bf16[128,768]{1,0:T(8,128)(2,1)S(1)}, u32[]{:S(2)}, u32[]{:S(2)}) collective-permute-start(bf16[128,768]{1,0:T(8,128)(2,1)S(1)} %get-tuple-element.77), channel_id=1, source_target_pairs={{0,2},{2,4},{4,6},{6,0},{1,3},{3,5},{5,7},{7,1},{8,10},{10,12},{12... | collective-permute-start | bytes 589832 | tf_op jit(solution)/shard_map/ppermute | solution.py:39
  83.9 20.5 %collective-permute-start.6 = (bf16[128,768]{1,0:T(8,128)(2,1)S(1)}, bf16[128,768]{1,0:T(8,128)(2,1)}, u32[]{:S(2)}, u32[]{:S(2)}) collective-permute-start(bf16[128,768]{1,0:T(8,128)(2,1)S(1)} %get-tuple-element.76), channel_id=1, source_target_pairs={{0,4},{2,6},{4,0},{6,2},{1,5},{3,7},{5,1},{7,3},{8,12},{10,14},{12... | collective-permute-start | bytes 589832 | tf_op jit(solution)/shard_map/ppermute | solution.py:39
  86.2 18.2 %collective-permute-start.7 = (bf16[128,768]{1,0:T(8,128)(2,1)S(1)}, bf16[128,768]{1,0:T(8,128)(2,1)}, u32[]{:S(2)}, u32[]{:S(2)}) collective-permute-start(bf16[128,768]{1,0:T(8,128)(2,1)S(1)} %get-tuple-element.75), channel_id=1, source_target_pairs={{0,6},{2,0},{4,2},{6,4},{1,7},{3,1},{5,3},{7,5},{8,14},{10,8},{12,... | collective-permute-start | bytes 589832 | tf_op jit(solution)/shard_map/ppermute | solution.py:39
  87.3 5.0 %collective-permute-start.3 = (bf16[80,768]{1,0:T(8,128)(2,1)S(1)}, bf16[80,768]{1,0:T(8,128)(2,1)S(1)}, u32[]{:S(2)}, u32[]{:S(2)}) collective-permute-start(bf16[80,768]{1,0:T(8,128)(2,1)S(1)} %get-tuple-element.46), channel_id=1, source_target_pairs={{0,8},{8,16},{16,24},{24,32},{32,40},{40,48},{48,56},{56,64},{64,7... | collective-permute-start | bytes 368648 | tf_op jit(solution)/shard_map/ppermute | solution.py:22
  90.4 6.0 %collective-permute-start.4 = (bf16[80,768]{1,0:T(8,128)(2,1)S(1)}, bf16[80,768]{1,0:T(8,128)(2,1)S(1)}, u32[]{:S(2)}, u32[]{:S(2)}) collective-permute-start(bf16[80,768]{1,0:T(8,128)(2,1)S(1)} %get-tuple-element.47), channel_id=1, source_target_pairs={{8,0},{16,8},{24,16},{32,24},{40,32},{48,40},{56,48},{64,56},{72,6... | collective-permute-start | bytes 368648 | tf_op jit(solution)/shard_map/ppermute | solution.py:22
  98.8 19.3 %all-to-all-start.3 = ((bf16[8,64,896]{2,1,0:T(8,128)(2,1)}), bf16[8,64,896]{2,1,0:T(8,128)(2,1)S(1)}, u32[]{:S(2)}, u32[]{:S(2)}) async-start(bf16[8,64,896]{2,1,0:T(8,128)(2,1)} %get-tuple-element.53), calls=%async_computation.3 | async-start | bytes 1835008 | tf_op jit(solution)/shard_map/all_to_all | solution.py:472
  105.5 12.6 %collective-permute-start.8 = (bf16[4,128,768]{2,1,0:T(8,128)(2,1)S(1)}, bf16[4,128,768]{2,1,0:T(8,128)(2,1)}, u32[]{:S(2)}, u32[]{:S(2)}) collective-permute-start(bf16[4,128,768]{2,1,0:T(8,128)(2,1)S(1)} %pad_maximum_fusion.near_ref), channel_id=1, source_target_pairs={{0,1},{1,0},{2,3},{3,2},{4,5},{5,4},{6,7},{7,6},{8,9},{9,8},{10,11... | collective-permute-start | bytes 2359304 | tf_op jit(solution)/shard_map/ppermute | solution.py:43
  121.4 20.1 %all-to-all-start.4 = ((bf16[4,8,24,640]{3,2,1,0:T(8,128)(2,1)}), bf16[4,8,24,640]{3,2,1,0:T(8,128)(2,1)S(1)}, u32[]{:S(2)}, u32[]{:S(2)}) async-start(bf16[4,8,24,640]{3,2,1,0:T(8,128)(2,1)} %shard_map.175), calls=%async_computation.4 | async-start | bytes 1966080 | tf_op jit(solution)/shard_map/all_to_all | solution.py:494
  127.3 10.0 %collective-permute-start.9 = (bf16[8,384]{1,0:T(8,128)(2,1)S(1)}, bf16[8,384]{1,0:T(8,128)(2,1)S(1)}, u32[]{:S(2)}, u32[]{:S(2)}) collective-permute-start(bf16[8,384]{1,0:T(8,128)(2,1)S(1)} %fusion.16), channel_id=1, source_target_pairs={{0,8},{1,9},{8,16},{9,17},{14,6},{15,7},{16,24},{17,25},{22,14},{2... | collective-permute-start | bytes 18440 | tf_op jit(solution)/shard_map/ppermute | solution.py:34
  138.2 3.2 %collective-permute-start.10 = (bf16[4,64,768]{2,1,0:T(8,128)(2,1)S(1)}, bf16[4,64,768]{2,1,0:T(8,128)(2,1)S(1)}, u32[]{:S(2)}, u32[]{:S(2)}) collective-permute-start(bf16[4,64,768]{2,1,0:T(8,128)(2,1)S(1)} %get-tuple-element.56), channel_id=1, source_target_pairs={{0,1},{1,0},{2,3},{3,2},{4,5},{5,4},{6,7},{7,6},{8,9},{9,8},{10,11... | collective-permute-start | bytes 1179656 | tf_op jit(solution)/shard_map/ppermute | solution.py:43
  142.4 16.6 %all-to-all-start.5 = ((bf16[8,24,640]{2,1,0:T(8,128)(2,1)}), bf16[8,24,640]{2,1,0:T(8,128)(2,1)S(1)}, u32[]{:S(2)}, u32[]{:S(2)}) async-start(bf16[8,24,640]{2,1,0:T(8,128)(2,1)} %reduce_sum.12), calls=%async_computation.5 | async-start | bytes 491520 | tf_op jit(solution)/shard_map/all_to_all | solution.py:496
  149.4 5.1 %collective-permute-start.11 = (bf16[64,768]{1,0:T(8,128)(2,1)S(1)}, bf16[64,768]{1,0:T(8,128)(2,1)S(1)}, u32[]{:S(2)}, u32[]{:S(2)}) collective-permute-start(bf16[64,768]{1,0:T(8,128)(2,1)S(1)} %get-tuple-element.73), channel_id=1, source_target_pairs={{0,2},{2,4},{4,6},{6,0},{1,3},{3,5},{5,7},{7,1},{8,10},{10,12},{12... | collective-permute-start | bytes 294920 | tf_op jit(solution)/shard_map/ppermute | solution.py:39
  149.5 8.3 %collective-permute-start.12 = (bf16[64,768]{1,0:T(8,128)(2,1)S(1)}, bf16[64,768]{1,0:T(8,128)(2,1)S(1)}, u32[]{:S(2)}, u32[]{:S(2)}) collective-permute-start(bf16[64,768]{1,0:T(8,128)(2,1)S(1)} %get-tuple-element.72), channel_id=1, source_target_pairs={{0,4},{2,6},{4,0},{6,2},{1,5},{3,7},{5,1},{7,3},{8,12},{10,14},{12... | collective-permute-start | bytes 294920 | tf_op jit(solution)/shard_map/ppermute | solution.py:39
  153.7 4.7 %collective-permute-start.13 = (bf16[64,768]{1,0:T(8,128)(2,1)S(1)}, bf16[64,768]{1,0:T(8,128)(2,1)S(1)}, u32[]{:S(2)}, u32[]{:S(2)}) collective-permute-start(bf16[64,768]{1,0:T(8,128)(2,1)S(1)} %get-tuple-element.71), channel_id=1, source_target_pairs={{0,6},{2,0},{4,2},{6,4},{1,7},{3,1},{5,3},{7,5},{8,14},{10,8},{12,... | collective-permute-start | bytes 294920 | tf_op jit(solution)/shard_map/ppermute | solution.py:39
Sparse Core Ops, SparseCore 0:
  10.4 30.3 all-gather.4
  48.7 31.6 all-gather.6
